TPU v7x, 32 devices: a whole 2x2x4 slice. The times are simulated.
32 devices in a mesh: grp: 2 (over y), pan: 4 (over z), seq: 4 (over x, core).
Axes of the slice: x: 2, y: 2, z: 4, core: 2. Of those that a mesh axis runs over, the one named last changes fastest.
Arguments:
- activations: bfloat16 [2048, 8192], P(('grp', 'seq'), 'pan'), parts along dimension 0, may hold values from -6 to 6
- out_grads: bfloat16 [2048, 8192], P(('grp', 'pan'), 'seq'), parts along dimension 0, may hold values from -6 to 6
- act_basis: bfloat16 [16384, 8192], P(('grp', 'pan'), 'seq'), parts along dimension 0, may hold values from -0.0625 to 0.0625
- grad_basis: bfloat16 [16384, 8192], P(('grp', 'seq'), 'pan'), parts along dimension 0, may hold values from -0.0625 to 0.0625
Outputs:
- correction: float32 [16384, 8192], P(('grp', 'pan'), 'seq'), parts along dimension 0
There are 2 independent parts, one for each index of `grp`. A program takes and returns all parts, laid end to end along the dimension named above; each array names one. Nothing has to cross between parts.
All inputs are finite; a program needn't handle non-finite values.
Results may differ from a plain program's by a relative error of at most 0.013.
Values may be sent and summed in bfloat16 or wider, within the bound.
A program may use at most 128 MiB of HBM per device.

v0:
```python
import math

import jax
import jax.numpy as jnp
from jax import lax
from jax.sharding import PartitionSpec as P

LEN = 128


def per_device(activations, out_grads, act_basis, grad_basis):
    full_acts = lax.all_gather(activations, "seq", axis=0, tiled=True)
    full_grads = lax.all_gather(out_grads, "pan", axis=0, tiled=True)
    token_count = full_acts.shape[0]
    rows_now = full_acts
    rot_acts = lax.psum(
        jnp.dot(rows_now, act_basis, preferred_element_type=jnp.float32).astype(jnp.bfloat16), "pan"
    )
    rows_now = full_grads
    rot_grads = lax.psum(
        jnp.dot(rows_now, grad_basis, preferred_element_type=jnp.float32).astype(jnp.bfloat16),
        "seq",
    )
    seq_count = token_count // LEN
    group_size = math.gcd(seq_count, 8)
    grad_groups = rot_grads.reshape(seq_count // group_size, group_size, LEN, rot_grads.shape[1])
    act_groups = rot_acts.reshape(seq_count // group_size, group_size, LEN, rot_acts.shape[1])

    def add_group(running, operands):
        grad_block, act_block = operands
        blocks = jnp.einsum(
            "gti,gtj->gij", grad_block, act_block, preferred_element_type=jnp.float32
        )
        return (running + jnp.sum(blocks * blocks, axis=0), None)

    start_sum = jnp.zeros((rot_grads.shape[1], rot_acts.shape[1]), jnp.float32)
    squares = lax.scan(add_group, start_sum, (grad_groups, act_groups))[0]
    return squares / (seq_count * LEN)


def solution(mesh):
    return jax.shard_map(
        per_device,
        mesh=mesh,
        in_specs=(
            P(("grp", "seq"), "pan"),
            P(("grp", "pan"), "seq"),
            P(("grp", "pan"), "seq"),
            P(("grp", "seq"), "pan"),
        ),
        out_specs=P(("grp", "pan"), "seq"),
        check_vma=False,
    )
```

profile of v0, /device:TPU:16, one launch (start us, length us, event | category | flops | bytes accessed | tf_op | source)
XLA Modules:
  0.0 418.3 jit_solution(6645065335032524466)
XLA Ops:
  6.5 0.0 all-gather.3.cloned.1.call-start
  6.5 0.7 all-gather.3.cloned.1.call-update
  7.3 0.0 all-gather.5.cloned.1.call-start
  7.3 0.7 all-gather.5.cloned.1.call-update
  8.0 0.0 all-reduce.3.cloned.1.call-start
  8.1 81.3 %all-gather.3.cloned.1.call-done = bf16[1024,2048]{1,0:T(8,128)(2,1)} async-done(((bf16[256,2048]{1,0:T(8,128)(2,1)}), bf16[1024,2048]{1,0:T(8,128)(2,1)}) %all-gather.3.cloned.1.call-update) | async-done | bytes 4194320 | tf_op jit(solution)/shard_map/all_gather | solution.py:13
  89.3 13.8 %convolution_convert_fusion.1 = bf16[1024,2048]{1,0:T(8,128)(2,1)} fusion(bf16[1024,2048]{1,0:T(8,128)(2,1)} %all-gather.3.cloned.1.call-done, bf16[2048,2048]{1,0:T(8,128)(2,1)} %param.7), kind=kOutput, calls=%fused_computation.3 | convolution fusion | flops 8592031744 | bytes 16777216 | tf_op jit(solution)/shard_map/dot_general | solution.py:21
  103.1 6.5 %copy.5 = bf16[8,128,2048]{1,2,0:T(8,128)(2,1)} copy(bf16[8,128,2048]{2,1,0:T(8,128)(2,1)} %bitcast.9) | data formatting | bytes 8388608 | tf_op jit(solution)/shard_map/while/body/jit(dynamic_index_in_dim)/squeeze | solution.py:37
  109.6 0.0 all-reduce.3.cloned.1.call-update
  109.7 0.2 all-reduce.5.cloned.1.call-start
  109.9 15.5 %all-gather.5.cloned.1.call-done = bf16[1024,2048]{1,0:T(8,128)(2,1)} async-done(((bf16[256,2048]{1,0:T(8,128)(2,1)}), bf16[1024,2048]{1,0:T(8,128)(2,1)}) %all-gather.5.cloned.1.call-update) | async-done | bytes 4194320 | tf_op jit(solution)/shard_map/all_gather | solution.py:12
  125.4 13.8 %convolution_convert_fusion = bf16[1024,2048]{1,0:T(8,128)(2,1)} fusion(bf16[1024,2048]{1,0:T(8,128)(2,1)} %all-gather.5.cloned.1.call-done, bf16[2048,2048]{1,0:T(8,128)(2,1)} %param.6), kind=kOutput, calls=%fused_computation.2 | convolution fusion | flops 8592031744 | bytes 16777216 | tf_op jit(solution)/shard_map/dot_general | solution.py:17
  139.2 0.0 all-reduce.5.cloned.1.call-update
  139.2 74.1 %all-reduce.3.cloned.1.call-done = bf16[8,128,2048]{1,2,0:T(8,128)(2,1)} async-done(((bf16[8,128,2048]{1,2,0:T(8,128)(2,1)}), bf16[8,128,2048]{1,2,0:T(8,128)(2,1)}) %all-reduce.3.cloned.1.call-update) | async-done | bytes 4194320 | tf_op jit(solution)/shard_map/psum | solution.py:20
  213.3 156.5 %all-reduce.5.cloned.1.call-done = bf16[8,128,2048]{2,1,0:T(8,128)(2,1)} async-done(((bf16[8,128,2048]{2,1,0:T(8,128)(2,1)}), bf16[8,128,2048]{2,1,0:T(8,128)(2,1)}) %all-reduce.5.cloned.1.call-update) | async-done | bytes 4194320 | tf_op jit(solution)/shard_map/psum | solution.py:16
  369.8 30.0 %multiply_reduce_fusion = f32[2048,2048]{1,0:T(8,128)} fusion(bf16[8,128,2048]{1,2,0:T(8,128)(2,1)} %all-reduce.3.cloned.1.call-done, bf16[8,128,2048]{2,1,0:T(8,128)(2,1)} %all-reduce.5.cloned.1.call-done), kind=kOutput, calls=%fused_computation | convolution fusion | flops 8652849152 | bytes 25165824 | tf_op jit(solution)/shard_map/while/body/eval_jaxpr/gti,gtj->gij/dot_general | solution.py:31
  399.8 12.0 %broadcast_multiply_fusion = f32[2048,2048]{1,0:T(8,128)} fusion(f32[2048,2048]{1,0:T(8,128)} %multiply_reduce_fusion), kind=kLoop, calls=%fused_computation.1 | loop fusion | flops 4194304 | bytes 33554432 | tf_op jit(solution)/shard_map/div | solution.py:38
Async XLA Ops:
  6.5 82.8 %all-gather.3.cloned.1.call-start = ((), (), s32[]{:S(2)}) async-start(), calls=%async_computation | async-start | bytes 5242880 | tf_op jit(solution)/shard_map/all_gather | solution.py:13
  7.3 118.1 %all-gather.5.cloned.1.call-start = ((), (), s32[]{:S(2)}) async-start(), calls=%async_computation.2 | async-start | bytes 5242880 | tf_op jit(solution)/shard_map/all_gather | solution.py:12
  8.0 205.3 %all-reduce.3.cloned.1.call-start = ((), (), s32[]{:S(2)}) async-start(), calls=%async_computation.1 | async-start | bytes 8388608 | tf_op jit(solution)/shard_map/psum | solution.py:20
  109.7 260.1 %all-reduce.5.cloned.1.call-start = ((), (), s32[]{:S(2)}) async-start(), calls=%async_computation.3 | async-start | bytes 8388608 | tf_op jit(solution)/shard_map/psum | solution.py:16
Sparse Core Ops, SparseCore 0:
  8.9 80.3 all-gather.2
  90.9 34.4 all-gather.4
  127.8 85.4 all-reduce.2
  215.6 154.1 all-reduce.4
where the time goes:
time: 421 us; the launch traced here: 418 us
  waiting for transfers between devices  329 us (78%)
  matrix products  57.5 us (14%)
  between operations  13.1 us (3%)
  other arithmetic  12 us (3%)
  local copies, waits for them, and re-layouts  6.53 us (2%)
    psum x1, waiting for transfers between devices, per_device(): lax.psum(jnp.dot(rows_now, act_basis, preferred_element_type=jnp.float32)...  157 us
    all_gather x1, waiting for transfers between devices, per_device(): full_grads = lax.all_gather(out_grads, 'pan', axis=0, tiled=True)  81.3 us
    psum x1, waiting for transfers between devices, per_device(): lax.psum(jnp.dot(rows_now, grad_basis, preferred_element_type=jnp.float32...  74.1 us
    dot_general x1, matrix products, add_group(): jnp.einsum('gti,gtj->gij', grad_block, act_block, preferred_element_type=...  30 us
    all_gather x1, waiting for transfers between devices, per_device(): full_acts = lax.all_gather(activations, 'seq', axis=0, tiled=True)  15.5 us
    dot_general x1, matrix products, per_device(): jnp.dot(rows_now, act_basis, preferred_element_type=jnp.float32)  13.8 us
    dot_general x1, matrix products, per_device(): jnp.dot(rows_now, grad_basis, preferred_element_type=jnp.float32)  13.8 us
    div x1, other arithmetic, per_device(): return squares / (seq_count * LEN)  12 us
  transfers between devices with their start and end apart: 4, of which 4 were waited for; matrix products, arithmetic and copies ran while one was open for 8% of the time, Pallas kernels for 0%

commit v1 on v0

v1 whole, which is shorter than its diff:
```python
import functools

import jax
import jax.numpy as jnp
from jax import lax
from jax.experimental import pallas as pl
from jax.experimental.pallas import tpu as pltpu
from jax.sharding import PartitionSpec as P

LEN = 128
SPLITS = 2


def take(array, index, rows):
    return lax.dynamic_slice_in_dim(array, index * rows, rows, 0)


def add(one, other):
    return (one.astype(jnp.float32) + other.astype(jnp.float32)).astype(one.dtype)


def line_gather(own, axis, n):
    me = lax.axis_index(axis)
    right, left = {}, {}
    going_right = going_left = own
    for t in range(1, n):
        going_right = lax.ppermute(going_right, axis, [(i, i + 1) for i in range(t - 1, n - 1)])
        going_left = lax.ppermute(going_left, axis, [(i, i - 1) for i in range(1, n - t + 1)])
        right[t], left[t] = going_right, going_left
    blocks = [own]
    for t in range(1, n):
        blocks.append(jnp.where(me >= t, right[t], left[n - t]))
    return blocks


def in_order(blocks, axis, n):
    me = lax.axis_index(axis)
    rows = blocks[0].shape[0]
    whole = jnp.zeros((n * rows, blocks[0].shape[1]), blocks[0].dtype)
    for t, block in enumerate(blocks):
        whole = lax.dynamic_update_slice_in_dim(whole, block, lax.rem(me - t + n, n) * rows, 0)
    return whole


def line_reduce_scatter(own, axis, n):
    me = lax.axis_index(axis)
    rows = own.shape[0] // n
    right, left = take(own, me + n - 1, rows), take(own, me - n + 1, rows)
    for d in range(n - 1, 0, -1):
        right = lax.ppermute(right, axis, [(i, i + 1) for i in range(n - d)])
        left = lax.ppermute(left, axis, [(i, i - 1) for i in range(d, n)])
        if d > 1:
            right = add(right, take(own, me - 1 + d, rows))
            left = add(left, take(own, me + 1 - d, rows))
    total = take(own, me, rows).astype(jnp.float32)
    return (total + right.astype(jnp.float32) + left.astype(jnp.float32)).astype(own.dtype)


def squares_kernel(sequences, tile, scale, grads_ref, acts_ref, out_ref):
    for column in range(0, out_ref.shape[1], tile):
        columns = pl.ds(column, tile)
        total = None
        for s in range(sequences):
            block = jnp.dot(
                grads_ref[:, pl.ds(s * LEN, LEN)],
                acts_ref[pl.ds(s * LEN, LEN), columns],
                preferred_element_type=jnp.float32,
            )
            total = block * block if total is None else total + block * block
        out_ref[:, columns] = total * scale


def squares(grads_t, acts):
    rows, tokens = grads_t.shape
    cols = acts.shape[1]
    step = min(256, rows)
    return pl.pallas_call(
        functools.partial(squares_kernel, tokens // LEN, min(512, cols), 1.0 / tokens),
        grid=(rows // step,),
        in_specs=[
            pl.BlockSpec((step, tokens), lambda i: (i, 0)),
            pl.BlockSpec((tokens, cols), lambda i: (0, 0)),
        ],
        out_specs=pl.BlockSpec((step, cols), lambda i: (i, 0)),
        out_shape=jax.ShapeDtypeStruct((rows, cols), jnp.float32),
        compiler_params=pltpu.CompilerParams(vmem_limit_bytes=40 * 1024 * 1024),
        cost_estimate=pl.CostEstimate(
            flops=2 * rows * cols * tokens,
            bytes_accessed=4 * rows * cols + 2 * tokens * (rows + cols),
            transcendentals=0,
        ),
    )(grads_t, acts)


def per_device(pan, activations, out_grads, act_basis, grad_basis):
    full_acts = lax.all_gather(activations, "seq", axis=0, tiled=True)
    full_grads = in_order(line_gather(out_grads, "pan", pan), "pan", pan)
    tokens = full_acts.shape[0]
    part = tokens // SPLITS
    act_parts = []
    for k in range(SPLITS):
        terms = jnp.dot(
            full_acts[k * part : (k + 1) * part], act_basis, preferred_element_type=jnp.float32
        ).astype(jnp.bfloat16)
        mine = line_reduce_scatter(terms, "pan", pan)
        act_parts.append(in_order(line_gather(mine, "pan", pan), "pan", pan))
    rot_acts = jnp.concatenate(act_parts, 0)
    terms_t = lax.dot_general(
        grad_basis, full_grads, (((0,), (1,)), ((), ())), preferred_element_type=jnp.float32
    ).astype(jnp.bfloat16)
    rot_grads_t = lax.psum(terms_t, "seq")
    return squares(rot_grads_t, rot_acts)


def solution(mesh):
    return jax.shard_map(
        functools.partial(per_device, mesh.shape["pan"]),
        mesh=mesh,
        in_specs=(
            P(("grp", "seq"), "pan"),
            P(("grp", "pan"), "seq"),
            P(("grp", "pan"), "seq"),
            P(("grp", "seq"), "pan"),
        ),
        out_specs=P(("grp", "pan"), "seq"),
        check_vma=False,
    )
```

time: 421 us -> 319 us (0.76)
  waiting for transfers between devices: 329 us -> 130 us
  starting transfers between devices: 0.3 us -> 88.2 us
  matrix products: 57.5 us -> 29.5 us
  Pallas kernels: 0 us -> 20.2 us
  other arithmetic: 12 us -> 25.2 us
    psum x2 -> x1, waiting for transfers between devices: 231 us -> 68.1 us  [per_device(): rot_grads_t = lax.psum(terms_t, 'seq')]
    ppermute x0 -> x30, starting transfers between devices: none -> 88.1 us  [the longest x6 31.9 us: line_reduce_scatter(): left = lax.ppermute(left, axis, [(i, i - 1) for i in range(d, n)])]
    all_gather x1 -> x0, waiting for transfers between devices: 81.3 us -> none  [per_device(): full_grads = lax.all_gather(out_grads, 'pan', axis=0, tiled=True)]
    ppermute x0 -> x30, waiting for transfers between devices: none -> 60.7 us  [the longest x9 48.6 us: line_gather(): lax.ppermute(going_left, axis, [(i, i - 1) for i in range(1, n - t + 1)])]
    dot_general x3, matrix products: 57.5 us -> 29.5 us  [the longest x2 16.8 us: per_device(): jnp.dot(full_acts[k * part:(k + 1) * part], act_basis, preferred_element_...]
    pallas_call x0 -> x1, Pallas kernels: none -> 20.2 us  [squares(): pl.pallas_call(functools.partial(squares_kernel, tokens // LEN, min(512,...]
    dynamic_update_slice x0 -> x11, other arithmetic: none -> 15.7 us  [in_order(): lax.dynamic_update_slice_in_dim(whole, block, lax.rem(me - t + n, n) * ro...]
    all_gather x1, waiting for transfers between devices: 15.5 us -> 0.01 us  [per_device(): full_acts = lax.all_gather(activations, 'seq', axis=0, tiled=True)]
  transfers between devices with their start and end apart: 4 -> 32, of which waited for: 4 -> 12; matrix products, arithmetic and copies ran while one was open for 8% -> 19% of each run, Pallas kernels for 0% -> 0%
where the time goes in v1:
time: 319 us; the launch traced here: 316 us
  waiting for transfers between devices  130 us (41%)
  starting transfers between devices  88.2 us (28%)
  matrix products  29.5 us (9%)
  other arithmetic  25.2 us (8%)
  Pallas kernels  20.2 us (6%)
  between operations  13.9 us (4%)
  local copies, waits for them, and re-layouts  9.73 us (3%)
    psum x1, waiting for transfers between devices, per_device(): rot_grads_t = lax.psum(terms_t, 'seq')  68.1 us
    ppermute x9, waiting for transfers between devices, line_gather(): lax.ppermute(going_left, axis, [(i, i - 1) for i in range(1, n - t + 1)])  48.6 us
    ppermute x6, starting transfers between devices, line_reduce_scatter(): left = lax.ppermute(left, axis, [(i, i - 1) for i in range(d, n)])  31.9 us
    ppermute x9, starting transfers between devices, line_gather(): lax.ppermute(going_left, axis, [(i, i - 1) for i in range(1, n - t + 1)])  27.5 us
    pallas_call x1, Pallas kernels, squares(): pl.pallas_call(functools.partial(squares_kernel, tokens // LEN, min(512,...  20.2 us
    ppermute x9, starting transfers between devices, line_gather(): lax.ppermute(going_right, axis, [(i, i + 1) for i in range(t - 1, n - 1)])  20 us
    dot_general x2, matrix products, per_device(): jnp.dot(full_acts[k * part:(k + 1) * part], act_basis, preferred_element_...  16.8 us
    dynamic_update_slice x11, other arithmetic, in_order(): lax.dynamic_update_slice_in_dim(whole, block, lax.rem(me - t + n, n) * ro...  15.7 us
  transfers between devices with their start and end apart: 32, of which 12 were waited for; matrix products, arithmetic and copies ran while one was open for 19% of the time, Pallas kernels for 0%

profile of v1, /device:TPU:16, one launch (start us, length us, event | category | flops | bytes accessed | tf_op | source)
XLA Modules:
  0.0 316.2 jit_solution(7606205767311573985)
XLA Ops:
  6.5 0.7 all-gather.2.cloned.1.call-update
  7.3 2.4 collective-permute-start.1
  9.7 3.5 %collective-permute-start = (bf16[256,2048]{1,0:T(8,128)(2,1)}, bf16[256,2048]{1,0:T(8,128)(2,1)}, u32[]{:S(2)}, u32[]{:S(2)}) collective-permute-start(bf16[256,2048]{1,0:T(8,128)(2,1)} %param.5), channel_id=1, source_target_pairs={{0,4},{4,8},{8,12},{1,5},{5,9},{9,13},{2,6},{6,10},{10,14},{3,7},{... | collective-permute-start | bytes 3145736 | tf_op jit(solution)/shard_map/ppermute | solution.py:27
  13.2 21.1 %collective-permute-done.1 = bf16[256,2048]{1,0:T(8,128)(2,1)S(1)} collective-permute-done((bf16[256,2048]{1,0:T(8,128)(2,1)}, bf16[256,2048]{1,0:T(8,128)(2,1)S(1)}, u32[]{:S(2)}, u32[]{:S(2)}) %collective-permute-start.1) | collective-permute-done | bytes 1048608 | tf_op jit(solution)/shard_map/ppermute | solution.py:28
  34.3 3.4 %collective-permute-start.2 = (bf16[256,2048]{1,0:T(8,128)(2,1)S(1)}, bf16[256,2048]{1,0:T(8,128)(2,1)}, u32[]{:S(2)}, u32[]{:S(2)}) collective-permute-start(bf16[256,2048]{1,0:T(8,128)(2,1)S(1)} %collective-permute-done.1), channel_id=1, source_target_pairs={{4,0},{8,4},{5,1},{9,5},{6,2},{10,6},{7,3},{11,7},{20,16},{24,20},... | collective-permute-start | bytes 3145736 | tf_op jit(solution)/shard_map/ppermute | solution.py:28
  37.7 2.3 collective-permute-start.4
  40.0 18.2 %collective-permute-done.2 = bf16[256,2048]{1,0:T(8,128)(2,1)} collective-permute-done((bf16[256,2048]{1,0:T(8,128)(2,1)S(1)}, bf16[256,2048]{1,0:T(8,128)(2,1)}, u32[]{:S(2)}, u32[]{:S(2)}) %collective-permute-start.2) | collective-permute-done | bytes 1048608 | tf_op jit(solution)/shard_map/ppermute | solution.py:28
  58.3 1.6 collective-permute-start.3
  59.9 8.7 %convolution_convert_fusion = bf16[512,2048]{1,0:T(8,128)(2,1)S(1)} fusion(bf16[2048,2048]{1,0:T(8,128)(2,1)} %param.6, bf16[1024,2048]{1,0:T(8,128)(2,1)} %all-gather.2.cloned.1.call-done), kind=kOutput, calls=%fused_computation.2 | convolution fusion | flops 4296015872 | bytes 12582912 | tf_op jit(solution)/shard_map/dot_general | solution.py:102
  68.7 0.7 collective-permute-start.18
  69.4 1.3 collective-permute-start.21
  70.7 8.2 %convolution_convert_fusion.1 = bf16[512,2048]{1,0:T(8,128)(2,1)S(1)} fusion(bf16[2048,2048]{1,0:T(8,128)(2,1)} %param.6, bf16[1024,2048]{1,0:T(8,128)(2,1)S(1)} %copy-done.8), kind=kOutput, calls=%fused_computation.3 | convolution fusion | flops 4296015872 | bytes 12582912 | tf_op jit(solution)/shard_map/dot_general | solution.py:102
  78.9 1.2 constant_dynamic-slice_fusion.3
  80.1 1.6 collective-permute-start.6
  81.7 1.3 collective-permute-start.9
  83.3 1.4 add_convert_fusion.4
  84.7 1.3 collective-permute-start.19
  86.0 7.8 %collective-permute-start.22 = (bf16[128,2048]{1,0:T(8,128)(2,1)}, bf16[128,2048]{1,0:T(8,128)(2,1)}, u32[]{:S(2)}, u32[]{:S(2)}) collective-permute-start(bf16[128,2048]{1,0:T(8,128)(2,1)} %get-tuple-element.18), channel_id=1, source_target_pairs={{8,4},{12,8},{9,5},{13,9},{10,6},{14,10},{11,7},{15,11},{24,20},{2... | collective-permute-start | bytes 1572872 | tf_op jit(solution)/shard_map/ppermute | solution.py:51
  93.8 2.5 broadcast_in_dim.3
  96.4 1.0 constant_dynamic-update-slice_fusion.2
  97.4 1.3 collective-permute-start.5
  98.8 1.6 add_convert_fusion.9
  100.4 1.3 collective-permute-start.7
  101.7 13.2 %collective-permute-start.10 = (bf16[128,2048]{1,0:T(8,128)(2,1)S(1)}, bf16[128,2048]{1,0:T(8,128)(2,1)S(1)}, u32[]{:S(2)}, u32[]{:S(2)}) collective-permute-start(bf16[128,2048]{1,0:T(8,128)(2,1)S(1)} %get-tuple-element.12), channel_id=1, source_target_pairs={{8,4},{12,8},{9,5},{13,9},{10,6},{14,10},{11,7},{15,11},{24,20},{2... | collective-permute-start | bytes 1572872 | tf_op jit(solution)/shard_map/ppermute | solution.py:51
  114.9 1.9 add_convert_fusion.3
  116.8 1.9 collective-permute-start.20
  118.7 3.9 %collective-permute-start.23 = (bf16[128,2048]{1,0:T(8,128)(2,1)S(1)}, bf16[128,2048]{1,0:T(8,128)(2,1)S(1)}, u32[]{:S(2)}, u32[]{:S(2)}) collective-permute-start(bf16[128,2048]{1,0:T(8,128)(2,1)S(1)} %get-tuple-element.16), channel_id=1, source_target_pairs={{4,0},{8,4},{12,8},{5,1},{9,5},{13,9},{6,2},{10,6},{14,10},{7,3},{... | collective-permute-start | bytes 1572872 | tf_op jit(solution)/shard_map/ppermute | solution.py:51
  122.7 2.6 select_dynamic-update-slice_fusion.2
  125.3 1.2 collective-permute-done.10
  126.9 1.9 collective-permute-start.8
  128.8 4.4 %collective-permute-start.11 = (bf16[128,2048]{1,0:T(8,128)(2,1)S(1)}, bf16[128,2048]{1,0:T(8,128)(2,1)S(1)}, u32[]{:S(2)}, u32[]{:S(2)}) collective-permute-start(bf16[128,2048]{1,0:T(8,128)(2,1)S(1)} %get-tuple-element.10), channel_id=1, source_target_pairs={{4,0},{8,4},{12,8},{5,1},{9,5},{13,9},{6,2},{10,6},{14,10},{7,3},{... | collective-permute-start | bytes 1572872 | tf_op jit(solution)/shard_map/ppermute | solution.py:51
  133.2 0.5 collective-permute-done.20
  133.8 4.0 %collective-permute-done.23 = bf16[128,2048]{1,0:T(8,128)(2,1)S(1)} collective-permute-done((bf16[128,2048]{1,0:T(8,128)(2,1)S(1)}, bf16[128,2048]{1,0:T(8,128)(2,1)S(1)}, u32[]{:S(2)}, u32[]{:S(2)}) %collective-permute-start.23) | collective-permute-done | bytes 524320 | tf_op jit(solution)/shard_map/ppermute | solution.py:51
  138.0 1.5 constant_dynamic-update-slice_fusion
  139.5 4.4 %collective-permute-start.25 = (bf16[128,2048]{1,0:T(8,128)(2,1)S(1)}, bf16[128,2048]{1,0:T(8,128)(2,1)S(1)}, u32[]{:S(2)}, u32[]{:S(2)}) collective-permute-start(bf16[128,2048]{1,0:T(8,128)(2,1)S(1)} %get-tuple-element.8), channel_id=1, source_target_pairs={{4,0},{8,4},{12,8},{5,1},{9,5},{13,9},{6,2},{10,6},{14,10},{7,3},{... | collective-permute-start | bytes 1572872 | tf_op jit(solution)/shard_map/ppermute | solution.py:28
  143.9 2.6 select_dynamic-update-slice_fusion.1
  146.5 2.2 collective-permute-start.24
  149.2 1.3 constant_dynamic-update-slice_fusion.1
  150.6 1.9 collective-permute-start.12
  152.5 4.4 %collective-permute-start.13 = (bf16[128,2048]{1,0:T(8,128)(2,1)S(1)}, bf16[128,2048]{1,0:T(8,128)(2,1)}, u32[]{:S(2)}, u32[]{:S(2)}) collective-permute-start(bf16[128,2048]{1,0:T(8,128)(2,1)S(1)} %get-tuple-element.6), channel_id=1, source_target_pairs={{4,0},{8,4},{12,8},{5,1},{9,5},{13,9},{6,2},{10,6},{14,10},{7,3},{... | collective-permute-start | bytes 1572872 | tf_op jit(solution)/shard_map/ppermute | solution.py:28
  156.9 3.3 %collective-permute-done.25 = bf16[128,2048]{1,0:T(8,128)(2,1)S(1)} collective-permute-done((bf16[128,2048]{1,0:T(8,128)(2,1)S(1)}, bf16[128,2048]{1,0:T(8,128)(2,1)S(1)}, u32[]{:S(2)}, u32[]{:S(2)}) %collective-permute-start.25) | collective-permute-done | bytes 524320 | tf_op jit(solution)/shard_map/ppermute | solution.py:28
  160.2 5.2 %collective-permute-start.26 = (bf16[128,2048]{1,0:T(8,128)(2,1)S(1)}, bf16[128,2048]{1,0:T(8,128)(2,1)}, u32[]{:S(2)}, u32[]{:S(2)}) collective-permute-start(bf16[128,2048]{1,0:T(8,128)(2,1)S(1)} %collective-permute-done.25), channel_id=1, source_target_pairs={{4,0},{8,4},{5,1},{9,5},{6,2},{10,6},{7,3},{11,7},{20,16},{24,20},... | collective-permute-start | bytes 1572872 | tf_op jit(solution)/shard_map/ppermute | solution.py:28
  165.4 1.4 select_dynamic-update-slice_fusion
  166.8 1.9 collective-permute-start.28
  168.7 4.0 %collective-permute-start.16 = (bf16[128,2048]{1,0:T(8,128)(2,1)}, bf16[128,2048]{1,0:T(8,128)(2,1)S(1)}, u32[]{:S(2)}, u32[]{:S(2)}) collective-permute-start(bf16[128,2048]{1,0:T(8,128)(2,1)} %collective-permute-done.12), channel_id=1, source_target_pairs={{4,8},{8,12},{5,9},{9,13},{6,10},{10,14},{7,11},{11,15},{20,24},{2... | collective-permute-start | bytes 1572872 | tf_op jit(solution)/shard_map/ppermute | solution.py:27
  172.7 4.0 %collective-permute-start.14 = (bf16[128,2048]{1,0:T(8,128)(2,1)}, bf16[128,2048]{1,0:T(8,128)(2,1)}, u32[]{:S(2)}, u32[]{:S(2)}) collective-permute-start(bf16[128,2048]{1,0:T(8,128)(2,1)} %collective-permute-done.13), channel_id=1, source_target_pairs={{4,0},{8,4},{5,1},{9,5},{6,2},{10,6},{7,3},{11,7},{20,16},{24,20},... | collective-permute-start | bytes 1572872 | tf_op jit(solution)/shard_map/ppermute | solution.py:28
  176.8 5.9 %collective-permute-done.26 = bf16[128,2048]{1,0:T(8,128)(2,1)} collective-permute-done((bf16[128,2048]{1,0:T(8,128)(2,1)S(1)}, bf16[128,2048]{1,0:T(8,128)(2,1)}, u32[]{:S(2)}, u32[]{:S(2)}) %collective-permute-start.26) | collective-permute-done | bytes 524320 | tf_op jit(solution)/shard_map/ppermute | solution.py:28
  182.7 1.5 collective-permute-start.27
  184.2 12.6 %convert_bitcast_fusion = bf16[2048,1024]{1,0:T(8,128)(2,1)} fusion(bf16[1024,2048]{1,0:T(8,128)(2,1)} %select_dynamic-update-slice_fusion, bf16[2048,2048]{1,0:T(8,128)(2,1)S(1)} %bitcast.7), kind=kOutput, calls=%fused_computation.1 | convolution fusion | flops 8592031744 | bytes 16777216 | tf_op jit(solution)/shard_map/dot_general | solution.py:108
  196.8 1.5 collective-permute-start.29
  198.3 1.3 collective-permute-start.17
  199.7 0.7 collective-permute-start.15
  200.4 2.0 select_dynamic-update-slice_fusion.5
  202.4 0.9 select_dynamic-update-slice_fusion.4
  203.3 1.2 select_dynamic-update-slice_fusion.8
  204.6 1.0 collective-permute-done.29
  205.7 0.9 select_dynamic-update-slice_fusion.3
  206.6 4.7 %collective-permute-done.17 = bf16[128,2048]{1,0:T(8,128)(2,1)S(1)} collective-permute-done((bf16[128,2048]{1,0:T(8,128)(2,1)S(1)}, bf16[128,2048]{1,0:T(8,128)(2,1)S(1)}, u32[]{:S(2)}, u32[]{:S(2)}) %collective-permute-start.17) | collective-permute-done | bytes 524320 | tf_op jit(solution)/shard_map/ppermute | solution.py:27
  211.3 1.2 select_dynamic-update-slice_fusion.6
  212.5 4.2 %pad_maximum_fusion.acts_ref = bf16[1024,2048]{1,0:T(8,128)(2,1)} fusion(bf16[512,2048]{1,0:T(8,128)(2,1)} %select_dynamic-update-slice_fusion.3, bf16[512,2048]{1,0:T(8,128)(2,1)S(1)} %select_dynamic-update-slice_fusion.6), kind=kLoop, calls=%fused_computation | loop fusion | flops 8388608 | bytes 8388608 | tf_op jit(solution)/shard_map/concatenate | solution.py:107
  216.6 68.1 %all-reduce.2.cloned.1.call-done.grads_ref = bf16[2048,1024]{1,0:T(8,128)(2,1)} async-done(((bf16[2048,1024]{1,0:T(8,128)(2,1)}), bf16[2048,1024]{1,0:T(8,128)(2,1)}) %all-reduce.2.cloned.1.call-update) | async-done | bytes 4194320 | tf_op jit(solution)/shard_map/psum | solution.py:111
  284.7 2.2 copy-done
  286.9 2.2 copy-done.1
  289.1 20.2 %shard_map.46 = f32[2048,2048]{1,0:T(8,128)} custom-call(bf16[2048,1024]{1,0:T(8,128)(2,1)S(1)} %copy-done.1, bf16[1024,2048]{1,0:T(8,128)(2,1)S(1)} %copy-done), custom_call_target="tpu_custom_call" | custom-call | flops 8589934592 | bytes 25165824 | tf_op jit(solution)/shard_map/pallas_call | solution.py:77
  (51 shorter events, 1.9 us)
Async XLA Ops:
  6.5 53.4 %all-gather.2.cloned.1.call-start = ((), (), s32[]{:S(2)}) async-start(), calls=%async_computation.1 | async-start | bytes 5242880 | tf_op jit(solution)/shard_map/all_gather | solution.py:96
  7.3 277.5 %all-reduce.2.cloned.1.call-start = ((), (), s32[]{:S(2)}) async-start(), calls=%async_computation | async-start | bytes 8388608 | tf_op jit(solution)/shard_map/psum | solution.py:111
  7.3 27.0 %collective-permute-start.1 = (bf16[256,2048]{1,0:T(8,128)(2,1)}, bf16[256,2048]{1,0:T(8,128)(2,1)S(1)}, u32[]{:S(2)}, u32[]{:S(2)}) collective-permute-start(bf16[256,2048]{1,0:T(8,128)(2,1)} %param.5), channel_id=1, source_target_pairs={{4,0},{8,4},{12,8},{5,1},{9,5},{13,9},{6,2},{10,6},{14,10},{7,3},{... | collective-permute-start | bytes 3145736 | tf_op jit(solution)/shard_map/ppermute | solution.py:28
  9.7 28.0 %collective-permute-start = (bf16[256,2048]{1,0:T(8,128)(2,1)}, bf16[256,2048]{1,0:T(8,128)(2,1)}, u32[]{:S(2)}, u32[]{:S(2)}) collective-permute-start(bf16[256,2048]{1,0:T(8,128)(2,1)} %param.5), channel_id=1, source_target_pairs={{0,4},{4,8},{8,12},{1,5},{5,9},{9,13},{2,6},{6,10},{10,14},{3,7},{... | collective-permute-start | bytes 3145736 | tf_op jit(solution)/shard_map/ppermute | solution.py:27
  34.3 24.0 %collective-permute-start.2 = (bf16[256,2048]{1,0:T(8,128)(2,1)S(1)}, bf16[256,2048]{1,0:T(8,128)(2,1)}, u32[]{:S(2)}, u32[]{:S(2)}) collective-permute-start(bf16[256,2048]{1,0:T(8,128)(2,1)S(1)} %collective-permute-done.1), channel_id=1, source_target_pairs={{4,0},{8,4},{5,1},{9,5},{6,2},{10,6},{7,3},{11,7},{20,16},{24,20},... | collective-permute-start | bytes 3145736 | tf_op jit(solution)/shard_map/ppermute | solution.py:28
  37.7 48.3 %collective-permute-start.4 = (bf16[256,2048]{1,0:T(8,128)(2,1)}, bf16[256,2048]{1,0:T(8,128)(2,1)}, u32[]{:S(2)}, u32[]{:S(2)}) collective-permute-start(bf16[256,2048]{1,0:T(8,128)(2,1)} %collective-permute-done), channel_id=1, source_target_pairs={{4,8},{8,12},{5,9},{9,13},{6,10},{10,14},{7,11},{11,15},{20,24},{2... | collective-permute-start | bytes 3145736 | tf_op jit(solution)/shard_map/ppermute | solution.py:27
  58.3 60.4 %collective-permute-start.3 = (bf16[256,2048]{1,0:T(8,128)(2,1)}, bf16[256,2048]{1,0:T(8,128)(2,1)}, u32[]{:S(2)}, u32[]{:S(2)}) collective-permute-start(bf16[256,2048]{1,0:T(8,128)(2,1)} %collective-permute-done.2), channel_id=1, source_target_pairs={{4,0},{5,1},{6,2},{7,3},{20,16},{21,17},{22,18},{23,19}} | collective-permute-start | bytes 3145736 | tf_op jit(solution)/shard_map/ppermute | solution.py:28
  59.9 10.8 %copy-start.8 = (bf16[1024,2048]{1,0:T(8,128)(2,1)S(1)}, bf16[1024,2048]{1,0:T(8,128)(2,1)}, u32[]{:S(2)}) copy-start(bf16[1024,2048]{1,0:T(8,128)(2,1)} %all-gather.2.cloned.1.call-done) | copy-start | bytes 12582916
  68.6 14.7 %copy-start.4 = (bf16[512,2048]{1,0:T(8,128)(2,1)}, bf16[512,2048]{1,0:T(8,128)(2,1)S(1)}, u32[]{:S(2)}) copy-start(bf16[512,2048]{1,0:T(8,128)(2,1)S(1)} %convolution_convert_fusion) | copy-start | bytes 6291460
  68.7 13.0 %collective-permute-start.18 = (bf16[128,2048]{1,0:T(8,128)(2,1)S(1)}, bf16[128,2048]{1,0:T(8,128)(2,1)S(1)}, u32[]{:S(2)}, u32[]{:S(2)}) collective-permute-start(bf16[128,2048]{1,0:T(8,128)(2,1)S(1)} %get-tuple-element.19), channel_id=1, source_target_pairs={{0,4},{1,5},{2,6},{3,7},{16,20},{17,21},{18,22},{19,23}} | collective-permute-start | bytes 1572872 | tf_op jit(solution)/shard_map/ppermute | solution.py:50
  69.4 13.9 %collective-permute-start.21 = (bf16[128,2048]{1,0:T(8,128)(2,1)S(1)}, bf16[128,2048]{1,0:T(8,128)(2,1)S(1)}, u32[]{:S(2)}, u32[]{:S(2)}) collective-permute-start(bf16[128,2048]{1,0:T(8,128)(2,1)S(1)} %get-tuple-element.20), channel_id=1, source_target_pairs={{12,8},{13,9},{14,10},{15,11},{28,24},{29,25},{30,26},{31,27}} | collective-permute-start | bytes 1572872 | tf_op jit(solution)/shard_map/ppermute | solution.py:51
  78.9 47.6 %copy-start.3 = (bf16[512,2048]{1,0:T(8,128)(2,1)}, bf16[512,2048]{1,0:T(8,128)(2,1)S(1)}, u32[]{:S(2)}) copy-start(bf16[512,2048]{1,0:T(8,128)(2,1)S(1)} %convolution_convert_fusion.1) | copy-start | bytes 6291460
  80.1 16.3 %copy-start.5 = (bf16[256,2048]{1,0:T(8,128)(2,1)S(1)}, bf16[256,2048]{1,0:T(8,128)(2,1)}, u32[]{:S(2)}) copy-start(bf16[256,2048]{1,0:T(8,128)(2,1)} %param.5) | copy-start | bytes 3145732
  80.1 17.4 %collective-permute-start.6 = (bf16[128,2048]{1,0:T(8,128)(2,1)}, bf16[128,2048]{1,0:T(8,128)(2,1)}, u32[]{:S(2)}, u32[]{:S(2)}) collective-permute-start(bf16[128,2048]{1,0:T(8,128)(2,1)} %get-tuple-element.13), channel_id=1, source_target_pairs={{0,4},{1,5},{2,6},{3,7},{16,20},{17,21},{18,22},{19,23}} | collective-permute-start | bytes 1572872 | tf_op jit(solution)/shard_map/ppermute | solution.py:50
  81.7 17.1 %collective-permute-start.9 = (bf16[128,2048]{1,0:T(8,128)(2,1)}, bf16[128,2048]{1,0:T(8,128)(2,1)}, u32[]{:S(2)}, u32[]{:S(2)}) collective-permute-start(bf16[128,2048]{1,0:T(8,128)(2,1)} %get-tuple-element.14), channel_id=1, source_target_pairs={{12,8},{13,9},{14,10},{15,11},{28,24},{29,25},{30,26},{31,27}} | collective-permute-start | bytes 1572872 | tf_op jit(solution)/shard_map/ppermute | solution.py:51
  84.7 17.0 %collective-permute-start.19 = (bf16[128,2048]{1,0:T(8,128)(2,1)}, bf16[128,2048]{1,0:T(8,128)(2,1)}, u32[]{:S(2)}, u32[]{:S(2)}) collective-permute-start(bf16[128,2048]{1,0:T(8,128)(2,1)} %get-tuple-element.17), channel_id=1, source_target_pairs={{0,4},{4,8},{1,5},{5,9},{2,6},{6,10},{3,7},{7,11},{16,20},{20,24},... | collective-permute-start | bytes 1572872 | tf_op jit(solution)/shard_map/ppermute | solution.py:50
  86.0 28.9 %collective-permute-start.22 = (bf16[128,2048]{1,0:T(8,128)(2,1)}, bf16[128,2048]{1,0:T(8,128)(2,1)}, u32[]{:S(2)}, u32[]{:S(2)}) collective-permute-start(bf16[128,2048]{1,0:T(8,128)(2,1)} %get-tuple-element.18), channel_id=1, source_target_pairs={{8,4},{12,8},{9,5},{13,9},{10,6},{14,10},{11,7},{15,11},{24,20},{2... | collective-permute-start | bytes 1572872 | tf_op jit(solution)/shard_map/ppermute | solution.py:51
  97.4 68.0 %collective-permute-start.5 = (bf16[256,2048]{1,0:T(8,128)(2,1)}, bf16[256,2048]{1,0:T(8,128)(2,1)S(1)}, u32[]{:S(2)}, u32[]{:S(2)}) collective-permute-start(bf16[256,2048]{1,0:T(8,128)(2,1)} %collective-permute-done.4), channel_id=1, source_target_pairs={{8,12},{9,13},{10,14},{11,15},{24,28},{25,29},{26,30},{27,31}} | collective-permute-start | bytes 3145736 | tf_op jit(solution)/shard_map/ppermute | solution.py:27
  100.4 24.9 %collective-permute-start.7 = (bf16[128,2048]{1,0:T(8,128)(2,1)S(1)}, bf16[128,2048]{1,0:T(8,128)(2,1)S(1)}, u32[]{:S(2)}, u32[]{:S(2)}) collective-permute-start(bf16[128,2048]{1,0:T(8,128)(2,1)S(1)} %get-tuple-element.11), channel_id=1, source_target_pairs={{0,4},{4,8},{1,5},{5,9},{2,6},{6,10},{3,7},{7,11},{16,20},{20,24},... | collective-permute-start | bytes 1572872 | tf_op jit(solution)/shard_map/ppermute | solution.py:50
  101.7 24.8 %collective-permute-start.10 = (bf16[128,2048]{1,0:T(8,128)(2,1)S(1)}, bf16[128,2048]{1,0:T(8,128)(2,1)S(1)}, u32[]{:S(2)}, u32[]{:S(2)}) collective-permute-start(bf16[128,2048]{1,0:T(8,128)(2,1)S(1)} %get-tuple-element.12), channel_id=1, source_target_pairs={{8,4},{12,8},{9,5},{13,9},{10,6},{14,10},{11,7},{15,11},{24,20},{2... | collective-permute-start | bytes 1572872 | tf_op jit(solution)/shard_map/ppermute | solution.py:51
  116.8 17.0 %collective-permute-start.20 = (bf16[128,2048]{1,0:T(8,128)(2,1)S(1)}, bf16[128,2048]{1,0:T(8,128)(2,1)S(1)}, u32[]{:S(2)}, u32[]{:S(2)}) collective-permute-start(bf16[128,2048]{1,0:T(8,128)(2,1)S(1)} %get-tuple-element.15), channel_id=1, source_target_pairs={{0,4},{4,8},{8,12},{1,5},{5,9},{9,13},{2,6},{6,10},{10,14},{3,7},{... | collective-permute-start | bytes 1572872 | tf_op jit(solution)/shard_map/ppermute | solution.py:50
  118.7 19.0 %collective-permute-start.23 = (bf16[128,2048]{1,0:T(8,128)(2,1)S(1)}, bf16[128,2048]{1,0:T(8,128)(2,1)S(1)}, u32[]{:S(2)}, u32[]{:S(2)}) collective-permute-start(bf16[128,2048]{1,0:T(8,128)(2,1)S(1)} %get-tuple-element.16), channel_id=1, source_target_pairs={{4,0},{8,4},{12,8},{5,1},{9,5},{13,9},{6,2},{10,6},{14,10},{7,3},{... | collective-permute-start | bytes 1572872 | tf_op jit(solution)/shard_map/ppermute | solution.py:51
  126.9 21.8 %collective-permute-start.8 = (bf16[128,2048]{1,0:T(8,128)(2,1)S(1)}, bf16[128,2048]{1,0:T(8,128)(2,1)S(1)}, u32[]{:S(2)}, u32[]{:S(2)}) collective-permute-start(bf16[128,2048]{1,0:T(8,128)(2,1)S(1)} %get-tuple-element.9), channel_id=1, source_target_pairs={{0,4},{4,8},{8,12},{1,5},{5,9},{9,13},{2,6},{6,10},{10,14},{3,7},{... | collective-permute-start | bytes 1572872 | tf_op jit(solution)/shard_map/ppermute | solution.py:50
  128.8 20.1 %collective-permute-start.11 = (bf16[128,2048]{1,0:T(8,128)(2,1)S(1)}, bf16[128,2048]{1,0:T(8,128)(2,1)S(1)}, u32[]{:S(2)}, u32[]{:S(2)}) collective-permute-start(bf16[128,2048]{1,0:T(8,128)(2,1)S(1)} %get-tuple-element.10), channel_id=1, source_target_pairs={{4,0},{8,4},{12,8},{5,1},{9,5},{13,9},{6,2},{10,6},{14,10},{7,3},{... | collective-permute-start | bytes 1572872 | tf_op jit(solution)/shard_map/ppermute | solution.py:51
  137.8 46.4 %slice-start = ((s8[8388608]{0:T(1024)(128)(4,1)}), s8[4194304]{0:T(1024)(128)(4,1)S(1)}, s32[]{:S(2)}) async-start(s8[8388608]{0:T(1024)(128)(4,1)} %bitcast.6), calls=%async_computation.2 | async-start | bytes 8388608
  139.5 27.3 %copy-start.2 = (bf16[512,2048]{1,0:T(8,128)(2,1)}, bf16[512,2048]{1,0:T(8,128)(2,1)S(1)}, u32[]{:S(2)}) copy-start(bf16[512,2048]{1,0:T(8,128)(2,1)S(1)} %get-tuple-element.7) | copy-start | bytes 6291460
  139.5 20.7 %collective-permute-start.25 = (bf16[128,2048]{1,0:T(8,128)(2,1)S(1)}, bf16[128,2048]{1,0:T(8,128)(2,1)S(1)}, u32[]{:S(2)}, u32[]{:S(2)}) collective-permute-start(bf16[128,2048]{1,0:T(8,128)(2,1)S(1)} %get-tuple-element.8), channel_id=1, source_target_pairs={{4,0},{8,4},{12,8},{5,1},{9,5},{13,9},{6,2},{10,6},{14,10},{7,3},{... | collective-permute-start | bytes 1572872 | tf_op jit(solution)/shard_map/ppermute | solution.py:28
  146.5 37.7 %slice-start.1 = ((s8[8388608]{0:T(1024)(128)(4,1)}), s8[4194304]{0:T(1024)(128)(4,1)S(1)}, s32[]{:S(2)}) async-start(s8[8388608]{0:T(1024)(128)(4,1)} %bitcast.6), calls=%async_computation.3 | async-start | bytes 8388608
  146.5 20.3 %collective-permute-start.24 = (bf16[128,2048]{1,0:T(8,128)(2,1)S(1)}, bf16[128,2048]{1,0:T(8,128)(2,1)}, u32[]{:S(2)}, u32[]{:S(2)}) collective-permute-start(bf16[128,2048]{1,0:T(8,128)(2,1)S(1)} %get-tuple-element.8), channel_id=1, source_target_pairs={{0,4},{4,8},{8,12},{1,5},{5,9},{9,13},{2,6},{6,10},{10,14},{3,7},{... | collective-permute-start | bytes 1572872 | tf_op jit(solution)/shard_map/ppermute | solution.py:27
  150.6 18.1 %collective-permute-start.12 = (bf16[128,2048]{1,0:T(8,128)(2,1)S(1)}, bf16[128,2048]{1,0:T(8,128)(2,1)}, u32[]{:S(2)}, u32[]{:S(2)}) collective-permute-start(bf16[128,2048]{1,0:T(8,128)(2,1)S(1)} %get-tuple-element.6), channel_id=1, source_target_pairs={{0,4},{4,8},{8,12},{1,5},{5,9},{9,13},{2,6},{6,10},{10,14},{3,7},{... | collective-permute-start | bytes 1572872 | tf_op jit(solution)/shard_map/ppermute | solution.py:27
  152.5 20.2 %collective-permute-start.13 = (bf16[128,2048]{1,0:T(8,128)(2,1)S(1)}, bf16[128,2048]{1,0:T(8,128)(2,1)}, u32[]{:S(2)}, u32[]{:S(2)}) collective-permute-start(bf16[128,2048]{1,0:T(8,128)(2,1)S(1)} %get-tuple-element.6), channel_id=1, source_target_pairs={{4,0},{8,4},{12,8},{5,1},{9,5},{13,9},{6,2},{10,6},{14,10},{7,3},{... | collective-permute-start | bytes 1572872 | tf_op jit(solution)/shard_map/ppermute | solution.py:28
  160.2 12.5 %copy-start.6 = (bf16[128,2048]{1,0:T(8,128)(2,1)}, bf16[128,2048]{1,0:T(8,128)(2,1)S(1)}, u32[]{:S(2)}) copy-start(bf16[128,2048]{1,0:T(8,128)(2,1)S(1)} %collective-permute-done.25) | copy-start | bytes 1572868
  160.2 22.5 %collective-permute-start.26 = (bf16[128,2048]{1,0:T(8,128)(2,1)S(1)}, bf16[128,2048]{1,0:T(8,128)(2,1)}, u32[]{:S(2)}, u32[]{:S(2)}) collective-permute-start(bf16[128,2048]{1,0:T(8,128)(2,1)S(1)} %collective-permute-done.25), channel_id=1, source_target_pairs={{4,0},{8,4},{5,1},{9,5},{6,2},{10,6},{7,3},{11,7},{20,16},{24,20},... | collective-permute-start | bytes 1572872 | tf_op jit(solution)/shard_map/ppermute | solution.py:28
  166.8 30.1 %collective-permute-start.28 = (bf16[128,2048]{1,0:T(8,128)(2,1)}, bf16[128,2048]{1,0:T(8,128)(2,1)S(1)}, u32[]{:S(2)}, u32[]{:S(2)}) collective-permute-start(bf16[128,2048]{1,0:T(8,128)(2,1)} %collective-permute-done.24), channel_id=1, source_target_pairs={{4,8},{8,12},{5,9},{9,13},{6,10},{10,14},{7,11},{11,15},{20,24},{2... | collective-permute-start | bytes 1572872 | tf_op jit(solution)/shard_map/ppermute | solution.py:27
  168.7 29.6 %collective-permute-start.16 = (bf16[128,2048]{1,0:T(8,128)(2,1)}, bf16[128,2048]{1,0:T(8,128)(2,1)S(1)}, u32[]{:S(2)}, u32[]{:S(2)}) collective-permute-start(bf16[128,2048]{1,0:T(8,128)(2,1)} %collective-permute-done.12), channel_id=1, source_target_pairs={{4,8},{8,12},{5,9},{9,13},{6,10},{10,14},{7,11},{11,15},{20,24},{2... | collective-permute-start | bytes 1572872 | tf_op jit(solution)/shard_map/ppermute | solution.py:27
  172.7 26.9 %collective-permute-start.14 = (bf16[128,2048]{1,0:T(8,128)(2,1)}, bf16[128,2048]{1,0:T(8,128)(2,1)}, u32[]{:S(2)}, u32[]{:S(2)}) collective-permute-start(bf16[128,2048]{1,0:T(8,128)(2,1)} %collective-permute-done.13), channel_id=1, source_target_pairs={{4,0},{8,4},{5,1},{9,5},{6,2},{10,6},{7,3},{11,7},{20,16},{24,20},... | collective-permute-start | bytes 1572872 | tf_op jit(solution)/shard_map/ppermute | solution.py:28
  182.7 17.7 %collective-permute-start.27 = (bf16[128,2048]{1,0:T(8,128)(2,1)}, bf16[128,2048]{1,0:T(8,128)(2,1)}, u32[]{:S(2)}, u32[]{:S(2)}) collective-permute-start(bf16[128,2048]{1,0:T(8,128)(2,1)} %collective-permute-done.26), channel_id=1, source_target_pairs={{4,0},{5,1},{6,2},{7,3},{20,16},{21,17},{22,18},{23,19}} | collective-permute-start | bytes 1572872 | tf_op jit(solution)/shard_map/ppermute | solution.py:28
  196.8 8.8 %copy-start.7 = (bf16[128,2048]{1,0:T(8,128)(2,1)S(1)}, bf16[128,2048]{1,0:T(8,128)(2,1)}, u32[]{:S(2)}) copy-start(bf16[128,2048]{1,0:T(8,128)(2,1)} %copy-done.6) | copy-start | bytes 1572868
  196.8 8.8 %collective-permute-start.29 = (bf16[128,2048]{1,0:T(8,128)(2,1)S(1)}, bf16[128,2048]{1,0:T(8,128)(2,1)S(1)}, u32[]{:S(2)}, u32[]{:S(2)}) collective-permute-start(bf16[128,2048]{1,0:T(8,128)(2,1)S(1)} %collective-permute-done.28), channel_id=1, source_target_pairs={{8,12},{9,13},{10,14},{11,15},{24,28},{25,29},{26,30},{27,31}} | collective-permute-start | bytes 1572872 | tf_op jit(solution)/shard_map/ppermute | solution.py:27
  198.3 13.0 %collective-permute-start.17 = (bf16[128,2048]{1,0:T(8,128)(2,1)S(1)}, bf16[128,2048]{1,0:T(8,128)(2,1)S(1)}, u32[]{:S(2)}, u32[]{:S(2)}) collective-permute-start(bf16[128,2048]{1,0:T(8,128)(2,1)S(1)} %collective-permute-done.16), channel_id=1, source_target_pairs={{8,12},{9,13},{10,14},{11,15},{24,28},{25,29},{26,30},{27,31}} | collective-permute-start | bytes 1572872 | tf_op jit(solution)/shard_map/ppermute | solution.py:27
  199.7 3.6 %collective-permute-start.15 = (bf16[128,2048]{1,0:T(8,128)(2,1)}, bf16[128,2048]{1,0:T(8,128)(2,1)S(1)}, u32[]{:S(2)}, u32[]{:S(2)}) collective-permute-start(bf16[128,2048]{1,0:T(8,128)(2,1)} %collective-permute-done.14), channel_id=1, source_target_pairs={{4,0},{5,1},{6,2},{7,3},{20,16},{21,17},{22,18},{23,19}} | collective-permute-start | bytes 1572872 | tf_op jit(solution)/shard_map/ppermute | solution.py:28
  284.7 2.2 copy-start
  286.9 2.2 copy-start.1
Sparse Core Ops, SparseCore 0:
  8.9 35.5 all-gather.1
  196.9 87.7 all-reduce.1

commit v2 on v1

v2 whole, which is shorter than its diff:
```python
import functools

import jax
import jax.numpy as jnp
from jax import lax
from jax.experimental import pallas as pl
from jax.experimental.pallas import tpu as pltpu
from jax.sharding import PartitionSpec as P

LEN = 128
SPLITS = 2


def take(array, index, rows):
    return lax.dynamic_slice_in_dim(array, index * rows, rows, 0)


def add(one, other):
    return (one.astype(jnp.float32) + other.astype(jnp.float32)).astype(one.dtype)


def line_gather(own, axis, n, ready=()):
    me = lax.axis_index(axis)
    right, left = {}, {}
    going_right = going_left = own
    for t in range(1, n):
        going_right = lax.ppermute(going_right, axis, [(i, i + 1) for i in range(t - 1, n - 1)])
        going_left = lax.ppermute(going_left, axis, [(i, i - 1) for i in range(1, n - t + 1)])
        if t == 2 and ready:
            going_right, going_left, ready = lax.optimization_barrier((going_right, going_left, ready))
        right[t], left[t] = going_right, going_left
    blocks = [own]
    for t in range(1, n):
        blocks.append(jnp.where(me >= t, right[t], left[n - t]))
    return blocks, ready


def in_order(blocks, axis, n):
    me = lax.axis_index(axis)
    rows = blocks[0].shape[0]
    whole = jnp.zeros((n * rows, blocks[0].shape[1]), blocks[0].dtype)
    for t, block in enumerate(blocks):
        whole = lax.dynamic_update_slice_in_dim(whole, block, lax.rem(me - t + n, n) * rows, 0)
    return whole


def line_reduce_scatter(own, axis, n, pin, when):
    me = lax.axis_index(axis)
    rows = own.shape[0] // n
    right, left = take(own, me + n - 1, rows), take(own, me - n + 1, rows)
    for d in range(n - 1, 0, -1):
        right = lax.ppermute(right, axis, [(i, i + 1) for i in range(n - d)])
        left = lax.ppermute(left, axis, [(i, i - 1) for i in range(d, n)])
        if d == when and pin is not None:
            right, left, pin = lax.optimization_barrier((right, left, pin))
        if d > 1:
            right = add(right, take(own, me - 1 + d, rows))
            left = add(left, take(own, me + 1 - d, rows))
    total = take(own, me, rows).astype(jnp.float32)
    return (total + right.astype(jnp.float32) + left.astype(jnp.float32)).astype(own.dtype), pin


def squares_kernel(sequences, tile, scale, *refs):
    grads_ref, acts_ref, *before, out_ref = refs
    for column in range(0, out_ref.shape[1], tile):
        columns = pl.ds(column, tile)
        total = None
        for s in range(sequences):
            block = jnp.dot(
                grads_ref[:, pl.ds(s * LEN, LEN)],
                acts_ref[pl.ds(s * LEN, LEN), columns],
                preferred_element_type=jnp.float32,
            )
            total = block * block if total is None else total + block * block
        total = total * scale
        out_ref[:, columns] = before[0][:, columns] + total if before else total


def squares(grads_t, acts, k, before):
    rows, tokens = grads_t.shape
    part, cols = acts.shape
    step = min(256, rows)
    out_spec = pl.BlockSpec((step, cols), lambda i: (i, 0))
    return pl.pallas_call(
        functools.partial(squares_kernel, part // LEN, min(512, cols), 1.0 / tokens),
        grid=(rows // step,),
        in_specs=[
            pl.BlockSpec((step, part), lambda i: (i, k)),
            pl.BlockSpec((part, cols), lambda i: (0, 0)),
        ]
        + [out_spec] * len(before),
        out_specs=out_spec,
        out_shape=jax.ShapeDtypeStruct((rows, cols), jnp.float32),
        input_output_aliases={2: 0} if before else {},
        compiler_params=pltpu.CompilerParams(vmem_limit_bytes=40 * 1024 * 1024),
        cost_estimate=pl.CostEstimate(
            flops=4 * rows * cols * part,
            bytes_accessed=4 * rows * cols * (1 + len(before)) + 2 * part * (rows + cols),
            transcendentals=0,
        ),
    )(grads_t, acts, *before)


def rotate_t(blocks, basis):
    rows = jnp.concatenate(blocks, 0)
    return lax.dot_general(
        basis, rows, (((0,), (1,)), ((), ())), preferred_element_type=jnp.float32
    ).astype(jnp.bfloat16)


def per_device(pan, activations, out_grads, act_basis, grad_basis):
    full_acts = lax.all_gather(activations, "seq", axis=0, tiled=True)
    tokens = full_acts.shape[0]
    part = tokens // SPLITS
    act_terms = [
        jnp.dot(
            full_acts[k * part : (k + 1) * part], act_basis, preferred_element_type=jnp.float32
        ).astype(jnp.bfloat16)
        for k in range(SPLITS)
    ]
    blocks, _ = line_gather(out_grads, "pan", pan, act_terms)
    by_arrival = sorted(range(pan), key=lambda t: (max(t, pan - t) if t else 0, t))
    groups = [by_arrival[: pan // 2], by_arrival[pan // 2 :]]
    terms_t = [rotate_t([blocks[t] for t in group], grad_basis) for group in groups]

    act_parts = []
    for k, terms in enumerate(act_terms):
        pin = terms_t[k] if k < 2 else None
        mine, pin = line_reduce_scatter(terms, "pan", pan, pin, pan - 1 - k)
        if k < 2:
            terms_t[k] = pin
        act_parts.append(mine)
    act_parts = [in_order(line_gather(mine, "pan", pan)[0], "pan", pan) for mine in act_parts]

    rows = out_grads.shape[0]
    me = lax.axis_index("pan")
    rot_grads_t = jnp.zeros((grad_basis.shape[1], tokens), jnp.bfloat16)
    first = lax.psum(terms_t[0], "seq")
    first, late = lax.optimization_barrier((first, terms_t[1]))
    for group, sums in zip(groups, [first, lax.psum(late, "seq")]):
        for place, t in enumerate(group):
            rot_grads_t = lax.dynamic_update_slice_in_dim(
                rot_grads_t,
                sums[:, place * rows : (place + 1) * rows],
                lax.rem(me - t + pan, pan) * rows,
                1,
            )
    out = []
    for k, acts in enumerate(act_parts):
        out = [squares(rot_grads_t, acts, k, out)]
    return out[0]


def solution(mesh):
    return jax.shard_map(
        functools.partial(per_device, mesh.shape["pan"]),
        mesh=mesh,
        in_specs=(
            P(("grp", "seq"), "pan"),
            P(("grp", "pan"), "seq"),
            P(("grp", "pan"), "seq"),
            P(("grp", "seq"), "pan"),
        ),
        out_specs=P(("grp", "pan"), "seq"),
        check_vma=False,
    )
```

time: 319 us -> 270 us (0.85)
  waiting for transfers between devices: 130 us -> 67.7 us
  Pallas kernels: 20.2 us -> 31.2 us
    psum x1 -> x2, waiting for transfers between devices: 68.1 us -> 15.7 us  [the longest x1 15.7 us: per_device(): lax.psum(late, 'seq')]
    ppermute x9, waiting for transfers between devices: 48.6 us -> 2.36 us  [line_gather(): lax.ppermute(going_left, axis, [(i, i - 1) for i in range(1, n - t + 1)])]
    ppermute x9, waiting for transfers between devices: 5.74 us -> 40.4 us  [line_gather(): lax.ppermute(going_right, axis, [(i, i + 1) for i in range(t - 1, n - 1)])]
    ppermute x6, starting transfers between devices: 31.9 us -> 20.7 us  [line_reduce_scatter(): left = lax.ppermute(left, axis, [(i, i - 1) for i in range(d, n)])]
    pallas_call x1 -> x2, Pallas kernels: 20.2 us -> 31.2 us  [squares(): pl.pallas_call(functools.partial(squares_kernel, part // LEN, min(512, co...]
    ppermute x9, starting transfers between devices: 20 us -> 26.6 us  [line_gather(): lax.ppermute(going_right, axis, [(i, i + 1) for i in range(t - 1, n - 1)])]
    convert_element_type x4, other arithmetic: 5.33 us -> 10.7 us  [add(): (one.astype(jnp.float32) + other.astype(jnp.float32)).astype(one.dtype)]
    dot_general x1 -> x2, matrix products: 12.6 us -> 17.6 us  [rotate_t(): lax.dot_general(basis, rows, (((0,), (1,)), ((), ())), preferred_element_...]
  transfers between devices with their start and end apart: 32 -> 33, of which waited for: 12 -> 9; matrix products, arithmetic and copies ran while one was open for 19% -> 26% of each run, Pallas kernels for 0% -> 5%
where the time goes in v2:
time: 270 us; the launch traced here: 269 us
  starting transfers between devices  86.9 us (32%)
  waiting for transfers between devices  67.7 us (25%)
  Pallas kernels  31.2 us (12%)
  matrix products  31.1 us (12%)
  other arithmetic  25.9 us (10%)
  between operations  13.7 us (5%)
  local copies, waits for them, and re-layouts  12.5 us (5%)
    ppermute x9, waiting for transfers between devices, line_gather(): lax.ppermute(going_right, axis, [(i, i + 1) for i in range(t - 1, n - 1)])  40.4 us
    pallas_call x2, Pallas kernels, squares(): pl.pallas_call(functools.partial(squares_kernel, part // LEN, min(512, co...  31.2 us
    ppermute x9, starting transfers between devices, line_gather(): lax.ppermute(going_left, axis, [(i, i - 1) for i in range(1, n - t + 1)])  30 us
    ppermute x9, starting transfers between devices, line_gather(): lax.ppermute(going_right, axis, [(i, i + 1) for i in range(t - 1, n - 1)])  26.6 us
    ppermute x6, starting transfers between devices, line_reduce_scatter(): left = lax.ppermute(left, axis, [(i, i - 1) for i in range(d, n)])  20.7 us
    dot_general x2, matrix products, rotate_t(): lax.dot_general(basis, rows, (((0,), (1,)), ((), ())), preferred_element_...  17.6 us
    psum x1, waiting for transfers between devices, per_device(): lax.psum(late, 'seq')  15.7 us
    dot_general x2, matrix products, per_device(): jnp.dot(full_acts[k * part:(k + 1) * part], act_basis, preferred_element_...  13.5 us
  transfers between devices with their start and end apart: 33, of which 9 were waited for; matrix products, arithmetic and copies ran while one was open for 26% of the time, Pallas kernels for 5%

profile of v2, /device:TPU:16, one launch (start us, length us, event | category | flops | bytes accessed | tf_op | source)
XLA Modules:
  0.0 268.9 jit_solution(10498471932572120312)
XLA Ops:
  7.3 3.5 %collective-permute-start.2 = (bf16[256,2048]{1,0:T(8,128)(2,1)}, bf16[256,2048]{1,0:T(8,128)(2,1)S(1)}, u32[]{:S(2)}, u32[]{:S(2)}) collective-permute-start(bf16[256,2048]{1,0:T(8,128)(2,1)} %param.5), channel_id=1, source_target_pairs={{0,4},{4,8},{8,12},{1,5},{5,9},{9,13},{2,6},{6,10},{10,14},{3,7},{... | collective-permute-start | bytes 3145736 | tf_op jit(solution)/shard_map/ppermute | solution.py:27
  10.8 2.4 collective-permute-start.4
  13.2 21.1 %collective-permute-done.2 = bf16[256,2048]{1,0:T(8,128)(2,1)S(1)} collective-permute-done((bf16[256,2048]{1,0:T(8,128)(2,1)}, bf16[256,2048]{1,0:T(8,128)(2,1)S(1)}, u32[]{:S(2)}, u32[]{:S(2)}) %collective-permute-start.2) | collective-permute-done | bytes 1048608 | tf_op jit(solution)/shard_map/ppermute | solution.py:27
  34.3 3.5 %collective-permute-start.3 = (bf16[256,2048]{1,0:T(8,128)(2,1)S(1)}, bf16[256,2048]{1,0:T(8,128)(2,1)}, u32[]{:S(2)}, u32[]{:S(2)}) collective-permute-start(bf16[256,2048]{1,0:T(8,128)(2,1)S(1)} %collective-permute-done.2), channel_id=1, source_target_pairs={{4,8},{8,12},{5,9},{9,13},{6,10},{10,14},{7,11},{11,15},{20,24},{2... | collective-permute-start | bytes 3145736 | tf_op jit(solution)/shard_map/ppermute | solution.py:27
  37.8 4.3 %collective-permute-start.5 = (bf16[256,2048]{1,0:T(8,128)(2,1)}, bf16[256,2048]{1,0:T(8,128)(2,1)}, u32[]{:S(2)}, u32[]{:S(2)}) collective-permute-start(bf16[256,2048]{1,0:T(8,128)(2,1)} %collective-permute-done.4), channel_id=1, source_target_pairs={{4,0},{8,4},{5,1},{9,5},{6,2},{10,6},{7,3},{11,7},{20,16},{24,20},... | collective-permute-start | bytes 3145736 | tf_op jit(solution)/shard_map/ppermute | solution.py:28
  42.1 2.4 all-gather.2.cloned.1.call-done
  44.5 8.7 %convolution_convert_fusion.3 = bf16[512,2048]{1,0:T(8,128)(2,1)S(1)} fusion(bf16[2048,2048]{1,0:T(8,128)(2,1)} %param.6, bf16[1024,2048]{1,0:T(8,128)(2,1)} %all-gather.2.cloned.1.call-done), kind=kOutput, calls=%fused_computation.3 | convolution fusion | flops 4296015872 | bytes 12582912 | tf_op jit(solution)/shard_map/dot_general | solution.py:116
  53.2 1.1 constant_dynamic-slice_fusion.2
  54.3 4.8 %convolution_convert_fusion.2 = bf16[512,2048]{1,0:T(8,128)(2,1)S(1)} fusion(bf16[2048,2048]{1,0:T(8,128)(2,1)S(1)} %copy-done.5, bf16[1024,2048]{1,0:T(8,128)(2,1)S(1)} %copy-done.6), kind=kOutput, calls=%fused_computation.2 | convolution fusion | flops 4296015872 | bytes 12582912 | tf_op jit(solution)/shard_map/dot_general | solution.py:116
  59.1 1.2 constant_dynamic-slice_fusion
  60.4 2.3 collective-permute-done.5
  62.8 1.3 collective-permute-start.1
  64.1 1.5 collective-permute-start
  65.6 1.3 collective-permute-start.8
  66.9 1.5 collective-permute-start.6
  68.4 7.1 %collective-permute-start.11 = (bf16[256,2048]{1,0:T(8,128)(2,1)}, bf16[256,2048]{1,0:T(8,128)(2,1)}, u32[]{:S(2)}, u32[]{:S(2)}) collective-permute-start(bf16[256,2048]{1,0:T(8,128)(2,1)} %collective-permute-done.3), channel_id=1, source_target_pairs={{8,12},{9,13},{10,14},{11,15},{24,28},{25,29},{26,30},{27,31}} | collective-permute-start | bytes 3145736 | tf_op jit(solution)/shard_map/ppermute | solution.py:27
  75.5 1.3 broadcast_select_fusion.2
  76.9 5.8 %fusion = bf16[2048,512]{1,0:T(8,128)(2,1)} fusion(bf16[2048,2048]{1,0:T(8,128)(2,1)S(1)} %bitcast.9, bf16[256,2048]{1,0:T(8,128)(2,1)S(1)} %broadcast_select_fusion.2, bf16[256,2048]{1,0:T(8,128)(2,1)S(1)} %copy-done.7), kind=kOutput, calls=%fused_computation.4 | convolution fusion | flops 4300210176 | bytes 12582912 | tf_op jit(solution)/shard_map/dot_general | solution.py:106
  82.7 2.9 %add_convert_fusion.4 = (bf16[128,2048]{1,0:T(8,128)(2,1)}, bf16[128,2048]{1,0:T(8,128)(2,1)}) fusion(bf16[128,2048]{1,0:T(8,128)(2,1)} %collective-permute-done, bf16[512,2048]{1,0:T(8,128)(2,1)} %copy-done.1, s32[]{:T(128)S(6)} %select_n.112, s32[]{:T(128)S(6)} %select_n.113, bf16[128,2048]{1,0:T(8,128)(2,1)} %collective-permute-done.1), kind=kLoop, calls=%fused_computation.20 | loop fusion | flops 2097152 | bytes 3145736 | tf_op jit(solution)/shard_map/convert_element_type | solution.py:19
  85.6 1.3 collective-permute-start.20
  86.9 4.6 %collective-permute-start.22 = (bf16[128,2048]{1,0:T(8,128)(2,1)}, bf16[128,2048]{1,0:T(8,128)(2,1)}, u32[]{:S(2)}, u32[]{:S(2)}) collective-permute-start(bf16[128,2048]{1,0:T(8,128)(2,1)} %get-tuple-element.32), channel_id=1, source_target_pairs={{8,4},{12,8},{9,5},{13,9},{10,6},{14,10},{11,7},{15,11},{24,20},{2... | collective-permute-start | bytes 1572872 | tf_op jit(solution)/shard_map/ppermute | solution.py:53
  91.6 0.9 collective-permute-start.10
  92.4 2.6 add_convert_fusion.8
  95.0 4.6 %collective-permute-start.9 = (bf16[128,2048]{1,0:T(8,128)(2,1)}, bf16[128,2048]{1,0:T(8,128)(2,1)}, u32[]{:S(2)}, u32[]{:S(2)}) collective-permute-start(bf16[128,2048]{1,0:T(8,128)(2,1)} %get-tuple-element.35), channel_id=1, source_target_pairs={{8,4},{12,8},{9,5},{13,9},{10,6},{14,10},{11,7},{15,11},{24,20},{2... | collective-permute-start | bytes 1572872 | tf_op jit(solution)/shard_map/ppermute | solution.py:53
  99.6 1.3 collective-permute-start.7
  100.9 3.2 %collective-permute-done.22 = bf16[128,2048]{1,0:T(8,128)(2,1)} collective-permute-done((bf16[128,2048]{1,0:T(8,128)(2,1)}, bf16[128,2048]{1,0:T(8,128)(2,1)}, u32[]{:S(2)}, u32[]{:S(2)}) %collective-permute-start.22) | collective-permute-done | bytes 524320 | tf_op jit(solution)/shard_map/ppermute | solution.py:53
  104.1 2.6 add_convert_fusion.3
  106.7 1.9 collective-permute-start.21
  108.6 4.6 %collective-permute-start.23 = (bf16[128,2048]{1,0:T(8,128)(2,1)}, bf16[128,2048]{1,0:T(8,128)(2,1)}, u32[]{:S(2)}, u32[]{:S(2)}) collective-permute-start(bf16[128,2048]{1,0:T(8,128)(2,1)} %get-tuple-element.30), channel_id=1, source_target_pairs={{4,0},{8,4},{12,8},{5,1},{9,5},{13,9},{6,2},{10,6},{14,10},{7,3},{... | collective-permute-start | bytes 1572872 | tf_op jit(solution)/shard_map/ppermute | solution.py:53
  113.2 1.4 broadcast_select_fusion
  114.7 11.8 %fusion.1 = bf16[2048,512]{1,0:T(8,128)(2,1)} fusion(bf16[2048,2048]{1,0:T(8,128)(2,1)} %param.7, bf16[256,2048]{1,0:T(8,128)(2,1)S(1)} %broadcast_select_fusion, bf16[256,2048]{1,0:T(8,128)(2,1)S(1)} %broadcast_select_fusion.1), kind=kOutput, calls=%fused_computation.5 | convolution fusion | flops 4300210176 | bytes 12582912 | tf_op jit(solution)/shard_map/dot_general | solution.py:106
  126.5 2.6 add_convert_fusion.7
  129.1 2.1 collective-permute-start.12
  131.2 4.4 %collective-permute-start.13 = (bf16[128,2048]{1,0:T(8,128)(2,1)}, bf16[128,2048]{1,0:T(8,128)(2,1)}, u32[]{:S(2)}, u32[]{:S(2)}) collective-permute-start(bf16[128,2048]{1,0:T(8,128)(2,1)} %get-tuple-element.34), channel_id=1, source_target_pairs={{4,0},{8,4},{12,8},{5,1},{9,5},{13,9},{6,2},{10,6},{14,10},{7,3},{... | collective-permute-start | bytes 1572872 | tf_op jit(solution)/shard_map/ppermute | solution.py:53
  135.7 1.7 broadcast.7.clone.1
  137.3 2.5 constant_dynamic-update-slice_fusion
  139.8 3.9 %collective-permute-start.25 = (bf16[128,2048]{1,0:T(8,128)(2,1)S(1)}, bf16[128,2048]{1,0:T(8,128)(2,1)}, u32[]{:S(2)}, u32[]{:S(2)}) collective-permute-start(bf16[128,2048]{1,0:T(8,128)(2,1)S(1)} %get-tuple-element.26), channel_id=1, source_target_pairs={{4,0},{8,4},{12,8},{5,1},{9,5},{13,9},{6,2},{10,6},{14,10},{7,3},{... | collective-permute-start | bytes 1572872 | tf_op jit(solution)/shard_map/ppermute | solution.py:28
  143.8 2.8 %collective-permute-done.13 = bf16[128,2048]{1,0:T(8,128)(2,1)} collective-permute-done((bf16[128,2048]{1,0:T(8,128)(2,1)}, bf16[128,2048]{1,0:T(8,128)(2,1)}, u32[]{:S(2)}, u32[]{:S(2)}) %collective-permute-start.13) | collective-permute-done | bytes 524320 | tf_op jit(solution)/shard_map/ppermute | solution.py:53
  146.9 1.5 constant_dynamic-update-slice_fusion.1
  148.4 2.1 collective-permute-start.14
  150.5 5.3 %collective-permute-start.15 = (bf16[128,2048]{1,0:T(8,128)(2,1)S(1)}, bf16[128,2048]{1,0:T(8,128)(2,1)S(1)}, u32[]{:S(2)}, u32[]{:S(2)}) collective-permute-start(bf16[128,2048]{1,0:T(8,128)(2,1)S(1)} %get-tuple-element.28), channel_id=1, source_target_pairs={{4,0},{8,4},{12,8},{5,1},{9,5},{13,9},{6,2},{10,6},{14,10},{7,3},{... | collective-permute-start | bytes 1572872 | tf_op jit(solution)/shard_map/ppermute | solution.py:28
  155.8 1.9 collective-permute-start.24
  157.7 5.5 %collective-permute-start.26 = (bf16[128,2048]{1,0:T(8,128)(2,1)}, bf16[128,2048]{1,0:T(8,128)(2,1)}, u32[]{:S(2)}, u32[]{:S(2)}) collective-permute-start(bf16[128,2048]{1,0:T(8,128)(2,1)} %collective-permute-done.25), channel_id=1, source_target_pairs={{4,0},{8,4},{5,1},{9,5},{6,2},{10,6},{7,3},{11,7},{20,16},{24,20},... | collective-permute-start | bytes 1572872 | tf_op jit(solution)/shard_map/ppermute | solution.py:28
  163.3 2.5 broadcast_in_dim.3
  165.8 1.1 slice_dynamic-update-slice_fusion.3
  166.8 1.1 slice_dynamic-update-slice_fusion.2
  167.9 1.9 collective-permute-start.18
  169.9 5.5 %collective-permute-start.16 = (bf16[128,2048]{1,0:T(8,128)(2,1)S(1)}, bf16[128,2048]{1,0:T(8,128)(2,1)}, u32[]{:S(2)}, u32[]{:S(2)}) collective-permute-start(bf16[128,2048]{1,0:T(8,128)(2,1)S(1)} %collective-permute-done.15), channel_id=1, source_target_pairs={{4,0},{8,4},{5,1},{9,5},{6,2},{10,6},{7,3},{11,7},{20,16},{24,20},... | collective-permute-start | bytes 1572872 | tf_op jit(solution)/shard_map/ppermute | solution.py:28
  175.4 2.5 collective-permute-done.24
  177.9 1.9 collective-permute-start.28
  179.9 1.5 collective-permute-start.27
  181.4 15.7 %all-reduce.5.cloned.1.call-done = bf16[2048,512]{1,0:T(8,128)(2,1)} async-done(((bf16[2048,512]{1,0:T(8,128)(2,1)}), bf16[2048,512]{1,0:T(8,128)(2,1)}) %all-reduce.5.cloned.1.call-update) | async-done | bytes 2097168 | tf_op jit(solution)/shard_map/psum | solution.py:140
  197.0 2.5 slice_dynamic-update-slice_fusion.1
  199.5 1.1 slice_dynamic-update-slice_fusion.refs_0_
  200.6 3.4 %collective-permute-start.19 = (bf16[128,2048]{1,0:T(8,128)(2,1)}, bf16[128,2048]{1,0:T(8,128)(2,1)S(1)}, u32[]{:S(2)}, u32[]{:S(2)}) collective-permute-start(bf16[128,2048]{1,0:T(8,128)(2,1)} %collective-permute-done.18), channel_id=1, source_target_pairs={{8,12},{9,13},{10,14},{11,15},{24,28},{25,29},{26,30},{27,31}} | collective-permute-start | bytes 1572872 | tf_op jit(solution)/shard_map/ppermute | solution.py:27
  204.7 1.3 collective-permute-start.29
  206.1 2.0 select_dynamic-update-slice_fusion.2
  208.0 2.0 select_dynamic-update-slice_fusion.1
  210.0 16.6 %collective-permute-done.29 = bf16[128,2048]{1,0:T(8,128)(2,1)S(1)} collective-permute-done((bf16[128,2048]{1,0:T(8,128)(2,1)}, bf16[128,2048]{1,0:T(8,128)(2,1)S(1)}, u32[]{:S(2)}, u32[]{:S(2)}) %collective-permute-start.29) | collective-permute-done | bytes 524320 | tf_op jit(solution)/shard_map/ppermute | solution.py:27
  226.6 2.0 select_dynamic-update-slice_fusion.refs_1_
  228.6 13.2 %shard_map.46.refs_2_ = f32[2048,2048]{1,0:T(8,128)} custom-call(bf16[2048,1024]{1,0:T(8,128)(2,1)} %slice_dynamic-update-slice_fusion.refs_0_, bf16[512,2048]{1,0:T(8,128)(2,1)} %select_dynamic-update-slice_fusion.refs_1_), custom_call_target="tpu_custom_call" | custom-call | flops 8589934592 | bytes 20971520 | tf_op jit(solution)/shard_map/pallas_call | solution.py:84
  241.9 1.2 select_dynamic-update-slice_fusion.5
  243.1 1.2 select_dynamic-update-slice_fusion.4
  244.4 18.0 %shard_map.47 = f32[2048,2048]{1,0:T(8,128)} custom-call(bf16[2048,1024]{1,0:T(8,128)(2,1)} %slice_dynamic-update-slice_fusion.refs_0_, bf16[512,2048]{1,0:T(8,128)(2,1)S(1)} %select_dynamic-update-slice_fusion.3.refs_1_, f32[2048,2048]{1,0:T(8,128)} %shard_map.46.refs_2_), custom_call_target="tpu_custom_call", output_to_operand_aliasing={{}: (2, {})} | custom-call | flops 8589934592 | bytes 37748736 | tf_op jit(solution)/shard_map/pallas_call | solution.py:84
  (56 shorter events, 2.3 us)
Async XLA Ops:
  6.5 38.0 %all-gather.2.cloned.1.call-start = ((), (), s32[]{:S(2)}) async-start(), calls=%async_computation | async-start | bytes 5242880 | tf_op jit(solution)/shard_map/all_gather | solution.py:112
  7.3 136.5 %all-reduce.3.cloned.1.call-start = ((), (), s32[]{:S(2)}) async-start(), calls=%async_computation.1 | async-start | bytes 4194304 | tf_op jit(solution)/shard_map/psum | solution.py:138
  7.3 27.0 %collective-permute-start.2 = (bf16[256,2048]{1,0:T(8,128)(2,1)}, bf16[256,2048]{1,0:T(8,128)(2,1)S(1)}, u32[]{:S(2)}, u32[]{:S(2)}) collective-permute-start(bf16[256,2048]{1,0:T(8,128)(2,1)} %param.5), channel_id=1, source_target_pairs={{0,4},{4,8},{8,12},{1,5},{5,9},{9,13},{2,6},{6,10},{10,14},{3,7},{... | collective-permute-start | bytes 3145736 | tf_op jit(solution)/shard_map/ppermute | solution.py:27
  10.8 27.0 %collective-permute-start.4 = (bf16[256,2048]{1,0:T(8,128)(2,1)}, bf16[256,2048]{1,0:T(8,128)(2,1)}, u32[]{:S(2)}, u32[]{:S(2)}) collective-permute-start(bf16[256,2048]{1,0:T(8,128)(2,1)} %param.5), channel_id=1, source_target_pairs={{4,0},{8,4},{12,8},{5,1},{9,5},{13,9},{6,2},{10,6},{14,10},{7,3},{... | collective-permute-start | bytes 3145736 | tf_op jit(solution)/shard_map/ppermute | solution.py:28
  34.3 26.1 %collective-permute-start.3 = (bf16[256,2048]{1,0:T(8,128)(2,1)S(1)}, bf16[256,2048]{1,0:T(8,128)(2,1)}, u32[]{:S(2)}, u32[]{:S(2)}) collective-permute-start(bf16[256,2048]{1,0:T(8,128)(2,1)S(1)} %collective-permute-done.2), channel_id=1, source_target_pairs={{4,8},{8,12},{5,9},{9,13},{6,10},{10,14},{7,11},{11,15},{20,24},{2... | collective-permute-start | bytes 3145736 | tf_op jit(solution)/shard_map/ppermute | solution.py:27
  37.8 25.0 %collective-permute-start.5 = (bf16[256,2048]{1,0:T(8,128)(2,1)}, bf16[256,2048]{1,0:T(8,128)(2,1)}, u32[]{:S(2)}, u32[]{:S(2)}) collective-permute-start(bf16[256,2048]{1,0:T(8,128)(2,1)} %collective-permute-done.4), channel_id=1, source_target_pairs={{4,0},{8,4},{5,1},{9,5},{6,2},{10,6},{7,3},{11,7},{20,16},{24,20},... | collective-permute-start | bytes 3145736 | tf_op jit(solution)/shard_map/ppermute | solution.py:28
  44.5 9.8 %copy-start.5 = (bf16[2048,2048]{1,0:T(8,128)(2,1)S(1)}, bf16[2048,2048]{1,0:T(8,128)(2,1)}, u32[]{:S(2)}) copy-start(bf16[2048,2048]{1,0:T(8,128)(2,1)} %param.6) | copy-start | bytes 25165828
  44.5 9.8 %copy-start.6 = (bf16[1024,2048]{1,0:T(8,128)(2,1)S(1)}, bf16[1024,2048]{1,0:T(8,128)(2,1)}, u32[]{:S(2)}) copy-start(bf16[1024,2048]{1,0:T(8,128)(2,1)} %all-gather.2.cloned.1.call-done) | copy-start | bytes 12582916
  53.2 5.9 %copy-start.1 = (bf16[512,2048]{1,0:T(8,128)(2,1)}, bf16[512,2048]{1,0:T(8,128)(2,1)S(1)}, u32[]{:S(2)}) copy-start(bf16[512,2048]{1,0:T(8,128)(2,1)S(1)} %convolution_convert_fusion.3) | copy-start | bytes 6291460
  53.2 23.7 %slice-start = ((s8[8388608]{0:T(1024)(128)(4,1)}), s8[4194304]{0:T(1024)(128)(4,1)S(1)}, s32[]{:S(2)}) async-start(s8[8388608]{0:T(1024)(128)(4,1)} %bitcast.8), calls=%async_computation.3 | async-start | bytes 8388608
  54.3 22.6 %slice-start.1 = ((s8[8388608]{0:T(1024)(128)(4,1)}), s8[4194304]{0:T(1024)(128)(4,1)S(1)}, s32[]{:S(2)}) async-start(s8[8388608]{0:T(1024)(128)(4,1)} %bitcast.8), calls=%async_computation.4 | async-start | bytes 8388608
  59.1 67.4 %copy-start = (bf16[512,2048]{1,0:T(8,128)(2,1)}, bf16[512,2048]{1,0:T(8,128)(2,1)S(1)}, u32[]{:S(2)}) copy-start(bf16[512,2048]{1,0:T(8,128)(2,1)S(1)} %convolution_convert_fusion.2) | copy-start | bytes 6291460
  60.3 16.6 %copy-start.7 = (bf16[256,2048]{1,0:T(8,128)(2,1)S(1)}, bf16[256,2048]{1,0:T(8,128)(2,1)}, u32[]{:S(2)}) copy-start(bf16[256,2048]{1,0:T(8,128)(2,1)} %param.5) | copy-start | bytes 3145732
  62.8 19.9 %collective-permute-start.1 = (bf16[128,2048]{1,0:T(8,128)(2,1)}, bf16[128,2048]{1,0:T(8,128)(2,1)}, u32[]{:S(2)}, u32[]{:S(2)}) collective-permute-start(bf16[128,2048]{1,0:T(8,128)(2,1)} %get-tuple-element.39), channel_id=1, source_target_pairs={{12,8},{13,9},{14,10},{15,11},{28,24},{29,25},{30,26},{31,27}} | collective-permute-start | bytes 1572872 | tf_op jit(solution)/shard_map/ppermute | solution.py:53
  64.1 18.6 %collective-permute-start = (bf16[128,2048]{1,0:T(8,128)(2,1)}, bf16[128,2048]{1,0:T(8,128)(2,1)}, u32[]{:S(2)}, u32[]{:S(2)}) collective-permute-start(bf16[128,2048]{1,0:T(8,128)(2,1)} %get-tuple-element.40), channel_id=1, source_target_pairs={{0,4},{1,5},{2,6},{3,7},{16,20},{17,21},{18,22},{19,23}} | collective-permute-start | bytes 1572872 | tf_op jit(solution)/shard_map/ppermute | solution.py:52
  65.6 26.0 %collective-permute-start.8 = (bf16[128,2048]{1,0:T(8,128)(2,1)}, bf16[128,2048]{1,0:T(8,128)(2,1)}, u32[]{:S(2)}, u32[]{:S(2)}) collective-permute-start(bf16[128,2048]{1,0:T(8,128)(2,1)} %get-tuple-element.37), channel_id=1, source_target_pairs={{12,8},{13,9},{14,10},{15,11},{28,24},{29,25},{30,26},{31,27}} | collective-permute-start | bytes 1572872 | tf_op jit(solution)/shard_map/ppermute | solution.py:53
  66.9 25.6 %collective-permute-start.6 = (bf16[128,2048]{1,0:T(8,128)(2,1)}, bf16[128,2048]{1,0:T(8,128)(2,1)}, u32[]{:S(2)}, u32[]{:S(2)}) collective-permute-start(bf16[128,2048]{1,0:T(8,128)(2,1)} %get-tuple-element.38), channel_id=1, source_target_pairs={{0,4},{1,5},{2,6},{3,7},{16,20},{17,21},{18,22},{19,23}} | collective-permute-start | bytes 1572872 | tf_op jit(solution)/shard_map/ppermute | solution.py:52
  68.4 40.3 %collective-permute-start.11 = (bf16[256,2048]{1,0:T(8,128)(2,1)}, bf16[256,2048]{1,0:T(8,128)(2,1)}, u32[]{:S(2)}, u32[]{:S(2)}) collective-permute-start(bf16[256,2048]{1,0:T(8,128)(2,1)} %collective-permute-done.3), channel_id=1, source_target_pairs={{8,12},{9,13},{10,14},{11,15},{24,28},{25,29},{26,30},{27,31}} | collective-permute-start | bytes 3145736 | tf_op jit(solution)/shard_map/ppermute | solution.py:27
  85.6 14.0 %collective-permute-start.20 = (bf16[128,2048]{1,0:T(8,128)(2,1)}, bf16[128,2048]{1,0:T(8,128)(2,1)}, u32[]{:S(2)}, u32[]{:S(2)}) collective-permute-start(bf16[128,2048]{1,0:T(8,128)(2,1)} %get-tuple-element.31), channel_id=1, source_target_pairs={{0,4},{4,8},{1,5},{5,9},{2,6},{6,10},{3,7},{7,11},{16,20},{20,24},... | collective-permute-start | bytes 1572872 | tf_op jit(solution)/shard_map/ppermute | solution.py:52
  86.9 17.2 %collective-permute-start.22 = (bf16[128,2048]{1,0:T(8,128)(2,1)}, bf16[128,2048]{1,0:T(8,128)(2,1)}, u32[]{:S(2)}, u32[]{:S(2)}) collective-permute-start(bf16[128,2048]{1,0:T(8,128)(2,1)} %get-tuple-element.32), channel_id=1, source_target_pairs={{8,4},{12,8},{9,5},{13,9},{10,6},{14,10},{11,7},{15,11},{24,20},{2... | collective-permute-start | bytes 1572872 | tf_op jit(solution)/shard_map/ppermute | solution.py:53
  91.5 105.6 %all-reduce.5.cloned.1.call-start = ((), (), s32[]{:S(2)}) async-start(), calls=%async_computation.2 | async-start | bytes 4194304 | tf_op jit(solution)/shard_map/psum | solution.py:140
  91.5 12.6 %copy-start.2 = (bf16[512,2048]{1,0:T(8,128)(2,1)S(1)}, bf16[512,2048]{1,0:T(8,128)(2,1)}, u32[]{:S(2)}) copy-start(bf16[512,2048]{1,0:T(8,128)(2,1)} %copy-done.1) | copy-start | bytes 6291460
  91.6 23.0 %collective-permute-start.10 = (bf16[256,2048]{1,0:T(8,128)(2,1)}, bf16[256,2048]{1,0:T(8,128)(2,1)S(1)}, u32[]{:S(2)}, u32[]{:S(2)}) collective-permute-start(bf16[256,2048]{1,0:T(8,128)(2,1)} %collective-permute-done.5), channel_id=1, source_target_pairs={{4,0},{5,1},{6,2},{7,3},{20,16},{21,17},{22,18},{23,19}} | collective-permute-start | bytes 3145736 | tf_op jit(solution)/shard_map/ppermute | solution.py:28
  95.0 31.5 %collective-permute-start.9 = (bf16[128,2048]{1,0:T(8,128)(2,1)}, bf16[128,2048]{1,0:T(8,128)(2,1)}, u32[]{:S(2)}, u32[]{:S(2)}) collective-permute-start(bf16[128,2048]{1,0:T(8,128)(2,1)} %get-tuple-element.35), channel_id=1, source_target_pairs={{8,4},{12,8},{9,5},{13,9},{10,6},{14,10},{11,7},{15,11},{24,20},{2... | collective-permute-start | bytes 1572872 | tf_op jit(solution)/shard_map/ppermute | solution.py:53
  99.6 26.9 %collective-permute-start.7 = (bf16[128,2048]{1,0:T(8,128)(2,1)}, bf16[128,2048]{1,0:T(8,128)(2,1)}, u32[]{:S(2)}, u32[]{:S(2)}) collective-permute-start(bf16[128,2048]{1,0:T(8,128)(2,1)} %get-tuple-element.36), channel_id=1, source_target_pairs={{0,4},{4,8},{1,5},{5,9},{2,6},{6,10},{3,7},{7,11},{16,20},{20,24},... | collective-permute-start | bytes 1572872 | tf_op jit(solution)/shard_map/ppermute | solution.py:52
  106.7 28.9 %collective-permute-start.21 = (bf16[128,2048]{1,0:T(8,128)(2,1)}, bf16[128,2048]{1,0:T(8,128)(2,1)}, u32[]{:S(2)}, u32[]{:S(2)}) collective-permute-start(bf16[128,2048]{1,0:T(8,128)(2,1)} %get-tuple-element.29), channel_id=1, source_target_pairs={{0,4},{4,8},{8,12},{1,5},{5,9},{9,13},{2,6},{6,10},{10,14},{3,7},{... | collective-permute-start | bytes 1572872 | tf_op jit(solution)/shard_map/ppermute | solution.py:52
  108.6 27.0 %collective-permute-start.23 = (bf16[128,2048]{1,0:T(8,128)(2,1)}, bf16[128,2048]{1,0:T(8,128)(2,1)}, u32[]{:S(2)}, u32[]{:S(2)}) collective-permute-start(bf16[128,2048]{1,0:T(8,128)(2,1)} %get-tuple-element.30), channel_id=1, source_target_pairs={{4,0},{8,4},{12,8},{5,1},{9,5},{13,9},{6,2},{10,6},{14,10},{7,3},{... | collective-permute-start | bytes 1572872 | tf_op jit(solution)/shard_map/ppermute | solution.py:53
  129.1 14.7 %collective-permute-start.12 = (bf16[128,2048]{1,0:T(8,128)(2,1)}, bf16[128,2048]{1,0:T(8,128)(2,1)S(1)}, u32[]{:S(2)}, u32[]{:S(2)}) collective-permute-start(bf16[128,2048]{1,0:T(8,128)(2,1)} %get-tuple-element.33), channel_id=1, source_target_pairs={{0,4},{4,8},{8,12},{1,5},{5,9},{9,13},{2,6},{6,10},{10,14},{3,7},{... | collective-permute-start | bytes 1572872 | tf_op jit(solution)/shard_map/ppermute | solution.py:52
  131.2 15.4 %collective-permute-start.13 = (bf16[128,2048]{1,0:T(8,128)(2,1)}, bf16[128,2048]{1,0:T(8,128)(2,1)}, u32[]{:S(2)}, u32[]{:S(2)}) collective-permute-start(bf16[128,2048]{1,0:T(8,128)(2,1)} %get-tuple-element.34), channel_id=1, source_target_pairs={{4,0},{8,4},{12,8},{5,1},{9,5},{13,9},{6,2},{10,6},{14,10},{7,3},{... | collective-permute-start | bytes 1572872 | tf_op jit(solution)/shard_map/ppermute | solution.py:53
  139.8 17.9 %collective-permute-start.25 = (bf16[128,2048]{1,0:T(8,128)(2,1)S(1)}, bf16[128,2048]{1,0:T(8,128)(2,1)}, u32[]{:S(2)}, u32[]{:S(2)}) collective-permute-start(bf16[128,2048]{1,0:T(8,128)(2,1)S(1)} %get-tuple-element.26), channel_id=1, source_target_pairs={{4,0},{8,4},{12,8},{5,1},{9,5},{13,9},{6,2},{10,6},{14,10},{7,3},{... | collective-permute-start | bytes 1572872 | tf_op jit(solution)/shard_map/ppermute | solution.py:28
  148.4 17.4 %copy-start.3 = (bf16[2048,512]{1,0:T(8,128)(2,1)S(1)}, bf16[2048,512]{1,0:T(8,128)(2,1)}, u32[]{:S(2)}) copy-start(bf16[2048,512]{1,0:T(8,128)(2,1)} %all-reduce.3.cloned.1.call-done) | copy-start | bytes 6291460
  148.4 19.5 %collective-permute-start.14 = (bf16[128,2048]{1,0:T(8,128)(2,1)S(1)}, bf16[128,2048]{1,0:T(8,128)(2,1)}, u32[]{:S(2)}, u32[]{:S(2)}) collective-permute-start(bf16[128,2048]{1,0:T(8,128)(2,1)S(1)} %get-tuple-element.28), channel_id=1, source_target_pairs={{0,4},{4,8},{8,12},{1,5},{5,9},{9,13},{2,6},{6,10},{10,14},{3,7},{... | collective-permute-start | bytes 1572872 | tf_op jit(solution)/shard_map/ppermute | solution.py:27
  150.5 19.4 %collective-permute-start.15 = (bf16[128,2048]{1,0:T(8,128)(2,1)S(1)}, bf16[128,2048]{1,0:T(8,128)(2,1)S(1)}, u32[]{:S(2)}, u32[]{:S(2)}) collective-permute-start(bf16[128,2048]{1,0:T(8,128)(2,1)S(1)} %get-tuple-element.28), channel_id=1, source_target_pairs={{4,0},{8,4},{12,8},{5,1},{9,5},{13,9},{6,2},{10,6},{14,10},{7,3},{... | collective-permute-start | bytes 1572872 | tf_op jit(solution)/shard_map/ppermute | solution.py:28
  155.8 22.1 %collective-permute-start.24 = (bf16[128,2048]{1,0:T(8,128)(2,1)S(1)}, bf16[128,2048]{1,0:T(8,128)(2,1)}, u32[]{:S(2)}, u32[]{:S(2)}) collective-permute-start(bf16[128,2048]{1,0:T(8,128)(2,1)S(1)} %get-tuple-element.26), channel_id=1, source_target_pairs={{0,4},{4,8},{8,12},{1,5},{5,9},{9,13},{2,6},{6,10},{10,14},{3,7},{... | collective-permute-start | bytes 1572872 | tf_op jit(solution)/shard_map/ppermute | solution.py:27
  157.7 22.1 %collective-permute-start.26 = (bf16[128,2048]{1,0:T(8,128)(2,1)}, bf16[128,2048]{1,0:T(8,128)(2,1)}, u32[]{:S(2)}, u32[]{:S(2)}) collective-permute-start(bf16[128,2048]{1,0:T(8,128)(2,1)} %collective-permute-done.25), channel_id=1, source_target_pairs={{4,0},{8,4},{5,1},{9,5},{6,2},{10,6},{7,3},{11,7},{20,16},{24,20},... | collective-permute-start | bytes 1572872 | tf_op jit(solution)/shard_map/ppermute | solution.py:28
  167.9 32.7 %collective-permute-start.18 = (bf16[128,2048]{1,0:T(8,128)(2,1)}, bf16[128,2048]{1,0:T(8,128)(2,1)}, u32[]{:S(2)}, u32[]{:S(2)}) collective-permute-start(bf16[128,2048]{1,0:T(8,128)(2,1)} %collective-permute-done.14), channel_id=1, source_target_pairs={{4,8},{8,12},{5,9},{9,13},{6,10},{10,14},{7,11},{11,15},{20,24},{2... | collective-permute-start | bytes 1572872 | tf_op jit(solution)/shard_map/ppermute | solution.py:27
  169.9 34.1 %collective-permute-start.16 = (bf16[128,2048]{1,0:T(8,128)(2,1)S(1)}, bf16[128,2048]{1,0:T(8,128)(2,1)}, u32[]{:S(2)}, u32[]{:S(2)}) collective-permute-start(bf16[128,2048]{1,0:T(8,128)(2,1)S(1)} %collective-permute-done.15), channel_id=1, source_target_pairs={{4,0},{8,4},{5,1},{9,5},{6,2},{10,6},{7,3},{11,7},{20,16},{24,20},... | collective-permute-start | bytes 1572872 | tf_op jit(solution)/shard_map/ppermute | solution.py:28
  177.9 26.8 %collective-permute-start.28 = (bf16[128,2048]{1,0:T(8,128)(2,1)}, bf16[128,2048]{1,0:T(8,128)(2,1)}, u32[]{:S(2)}, u32[]{:S(2)}) collective-permute-start(bf16[128,2048]{1,0:T(8,128)(2,1)} %collective-permute-done.24), channel_id=1, source_target_pairs={{4,8},{8,12},{5,9},{9,13},{6,10},{10,14},{7,11},{11,15},{20,24},{2... | collective-permute-start | bytes 1572872 | tf_op jit(solution)/shard_map/ppermute | solution.py:27
  179.9 26.2 %collective-permute-start.27 = (bf16[128,2048]{1,0:T(8,128)(2,1)}, bf16[128,2048]{1,0:T(8,128)(2,1)}, u32[]{:S(2)}, u32[]{:S(2)}) collective-permute-start(bf16[128,2048]{1,0:T(8,128)(2,1)} %collective-permute-done.26), channel_id=1, source_target_pairs={{4,0},{5,1},{6,2},{7,3},{20,16},{21,17},{22,18},{23,19}} | collective-permute-start | bytes 1572872 | tf_op jit(solution)/shard_map/ppermute | solution.py:28
  197.0 2.5 copy-start.4
  200.6 43.6 %collective-permute-start.19 = (bf16[128,2048]{1,0:T(8,128)(2,1)}, bf16[128,2048]{1,0:T(8,128)(2,1)S(1)}, u32[]{:S(2)}, u32[]{:S(2)}) collective-permute-start(bf16[128,2048]{1,0:T(8,128)(2,1)} %collective-permute-done.18), channel_id=1, source_target_pairs={{8,12},{9,13},{10,14},{11,15},{24,28},{25,29},{26,30},{27,31}} | collective-permute-start | bytes 1572872 | tf_op jit(solution)/shard_map/ppermute | solution.py:27
  204.0 37.9 %collective-permute-start.17 = (bf16[128,2048]{1,0:T(8,128)(2,1)}, bf16[128,2048]{1,0:T(8,128)(2,1)S(1)}, u32[]{:S(2)}, u32[]{:S(2)}) collective-permute-start(bf16[128,2048]{1,0:T(8,128)(2,1)} %collective-permute-done.16), channel_id=1, source_target_pairs={{4,0},{5,1},{6,2},{7,3},{20,16},{21,17},{22,18},{23,19}} | collective-permute-start | bytes 1572872 | tf_op jit(solution)/shard_map/ppermute | solution.py:28
  204.7 21.9 %collective-permute-start.29 = (bf16[128,2048]{1,0:T(8,128)(2,1)}, bf16[128,2048]{1,0:T(8,128)(2,1)S(1)}, u32[]{:S(2)}, u32[]{:S(2)}) collective-permute-start(bf16[128,2048]{1,0:T(8,128)(2,1)} %collective-permute-done.28), channel_id=1, source_target_pairs={{8,12},{9,13},{10,14},{11,15},{24,28},{25,29},{26,30},{27,31}} | collective-permute-start | bytes 1572872 | tf_op jit(solution)/shard_map/ppermute | solution.py:27
Sparse Core Ops, SparseCore 0:
  8.9 35.5 all-gather.1
  91.6 51.4 all-reduce.2
  145.6 51.4 all-reduce.4

commit v3 on v2

--- a/solution.py
+++ b/solution.py
@@ -60,45 +60,41 @@
     return (total + right.astype(jnp.float32) + left.astype(jnp.float32)).astype(own.dtype), pin
 
 
-def squares_kernel(sequences, tile, scale, *refs):
-    grads_ref, acts_ref, *before, out_ref = refs
+def squares_kernel(tile, scale, grads_ref, *refs):
+    *parts, out_ref = refs
+    part = parts[0].shape[0]
     for column in range(0, out_ref.shape[1], tile):
         columns = pl.ds(column, tile)
         total = None
-        for s in range(sequences):
-            block = jnp.dot(
-                grads_ref[:, pl.ds(s * LEN, LEN)],
-                acts_ref[pl.ds(s * LEN, LEN), columns],
-                preferred_element_type=jnp.float32,
-            )
-            total = block * block if total is None else total + block * block
-        total = total * scale
-        out_ref[:, columns] = before[0][:, columns] + total if before else total
+        for k, acts_ref in enumerate(parts):
+            for s in range(0, part, LEN):
+                block = jnp.dot(
+                    grads_ref[:, pl.ds(k * part + s, LEN)],
+                    acts_ref[pl.ds(s, LEN), columns],
+                    preferred_element_type=jnp.float32,
+                )
+                total = block * block if total is None else total + block * block
+        out_ref[:, columns] = total * scale
 
 
-def squares(grads_t, acts, k, before):
+def squares(grads_t, act_parts):
     rows, tokens = grads_t.shape
-    part, cols = acts.shape
+    part, cols = act_parts[0].shape
     step = min(256, rows)
-    out_spec = pl.BlockSpec((step, cols), lambda i: (i, 0))
     return pl.pallas_call(
-        functools.partial(squares_kernel, part // LEN, min(512, cols), 1.0 / tokens),
+        functools.partial(squares_kernel, min(512, cols), 1.0 / tokens),
         grid=(rows // step,),
-        in_specs=[
-            pl.BlockSpec((step, part), lambda i: (i, k)),
-            pl.BlockSpec((part, cols), lambda i: (0, 0)),
-        ]
-        + [out_spec] * len(before),
-        out_specs=out_spec,
+        in_specs=[pl.BlockSpec((step, tokens), lambda i: (i, 0))]
+        + [pl.BlockSpec((part, cols), lambda i: (0, 0))] * len(act_parts),
+        out_specs=pl.BlockSpec((step, cols), lambda i: (i, 0)),
         out_shape=jax.ShapeDtypeStruct((rows, cols), jnp.float32),
-        input_output_aliases={2: 0} if before else {},
         compiler_params=pltpu.CompilerParams(vmem_limit_bytes=40 * 1024 * 1024),
         cost_estimate=pl.CostEstimate(
-            flops=4 * rows * cols * part,
-            bytes_accessed=4 * rows * cols * (1 + len(before)) + 2 * part * (rows + cols),
+            flops=4 * rows * cols * tokens,
+            bytes_accessed=4 * rows * cols + 2 * tokens * (rows + cols),
             transcendentals=0,
         ),
-    )(grads_t, acts, *before)
+    )(grads_t, *act_parts)
 
 
 def rotate_t(blocks, basis):
@@ -137,7 +133,8 @@
     rot_grads_t = jnp.zeros((grad_basis.shape[1], tokens), jnp.bfloat16)
     first = lax.psum(terms_t[0], "seq")
     first, late = lax.optimization_barrier((first, terms_t[1]))
-    for group, sums in zip(groups, [first, lax.psum(late, "seq")]):
+    second, act_parts = lax.optimization_barrier((lax.psum(late, "seq"), act_parts))
+    for group, sums in zip(groups, [first, second]):
         for place, t in enumerate(group):
             rot_grads_t = lax.dynamic_update_slice_in_dim(
                 rot_grads_t,
@@ -145,10 +142,7 @@
                 lax.rem(me - t + pan, pan) * rows,
                 1,
             )
-    out = []
-    for k, acts in enumerate(act_parts):
-        out = [squares(rot_grads_t, acts, k, out)]
-    return out[0]
+    return squares(rot_grads_t, act_parts)
 
 
 def solution(mesh):

time: 270 us -> 252 us (0.933)
  Pallas kernels: 31.2 us -> 20.2 us
  other arithmetic: 25.9 us -> 20.5 us
    pallas_call x2 -> x1, Pallas kernels: 31.2 us -> 20.2 us  [squares(): pl.pallas_call(functools.partial(squares_kernel, min(512, cols), 1.0 / to...]
    ppermute x9, waiting for transfers between devices: 2.36 us -> 12 us  [line_gather(): lax.ppermute(going_left, axis, [(i, i - 1) for i in range(1, n - t + 1)])]
    psum x1, waiting for transfers between devices: 15.7 us -> 8.59 us  [per_device(): lax.psum(late, 'seq')]
    ppermute x9, waiting for transfers between devices: 40.4 us -> 35.3 us  [line_gather(): lax.ppermute(going_right, axis, [(i, i + 1) for i in range(t - 1, n - 1)])]
    dynamic_update_slice x8, other arithmetic: 12.4 us -> 8.08 us  [in_order(): lax.dynamic_update_slice_in_dim(whole, block, lax.rem(me - t + n, n) * ro...]
    ppermute x9, starting transfers between devices: 30 us -> 25.9 us  [line_gather(): lax.ppermute(going_left, axis, [(i, i - 1) for i in range(1, n - t + 1)])]
    unnamed x20 -> x30, local copies, waits for them, and re-layouts: 0.04 us -> 3.6 us
  transfers between devices with their start and end apart: 33 -> 33, of which waited for: 9 -> 13; matrix products, arithmetic and copies ran while one was open for 26% -> 22% of each run, Pallas kernels for 5% -> 0%
where the time goes in v3:
time: 252 us; the launch traced here: 249 us
  starting transfers between devices  85.4 us (34%)
  waiting for transfers between devices  65.9 us (26%)
  matrix products  31.1 us (12%)
  other arithmetic  20.5 us (8%)
  Pallas kernels  20.2 us (8%)
  between operations  13.8 us (5%)
  local copies, waits for them, and re-layouts  11.8 us (5%)
    ppermute x9, waiting for transfers between devices, line_gather(): lax.ppermute(going_right, axis, [(i, i + 1) for i in range(t - 1, n - 1)])  35.3 us
    ppermute x9, starting transfers between devices, line_gather(): lax.ppermute(going_right, axis, [(i, i + 1) for i in range(t - 1, n - 1)])  29.1 us
    ppermute x9, starting transfers between devices, line_gather(): lax.ppermute(going_left, axis, [(i, i - 1) for i in range(1, n - t + 1)])  25.9 us
    ppermute x6, starting transfers between devices, line_reduce_scatter(): left = lax.ppermute(left, axis, [(i, i - 1) for i in range(d, n)])  20.7 us
    pallas_call x1, Pallas kernels, squares(): pl.pallas_call(functools.partial(squares_kernel, min(512, cols), 1.0 / to...  20.2 us
    dot_general x2, matrix products, rotate_t(): lax.dot_general(basis, rows, (((0,), (1,)), ((), ())), preferred_element_...  17.6 us
    dot_general x2, matrix products, per_device(): jnp.dot(full_acts[k * part:(k + 1) * part], act_basis, preferred_element_...  13.5 us
    ppermute x9, waiting for transfers between devices, line_gather(): lax.ppermute(going_left, axis, [(i, i - 1) for i in range(1, n - t + 1)])  12 us
  transfers between devices with their start and end apart: 33, of which 13 were waited for; matrix products, arithmetic and copies ran while one was open for 22% of the time, Pallas kernels for 0%

profile of v3, /device:TPU:16, one launch (start us, length us, event | category | flops | bytes accessed | tf_op | source)
XLA Modules:
  0.0 248.7 jit_solution(11587232044704627428)
XLA Ops:
  6.5 0.7 all-gather.2.cloned.1.call-update
  7.3 3.5 %collective-permute-start.2 = (bf16[256,2048]{1,0:T(8,128)(2,1)}, bf16[256,2048]{1,0:T(8,128)(2,1)S(1)}, u32[]{:S(2)}, u32[]{:S(2)}) collective-permute-start(bf16[256,2048]{1,0:T(8,128)(2,1)} %param.5), channel_id=1, source_target_pairs={{0,4},{4,8},{8,12},{1,5},{5,9},{9,13},{2,6},{6,10},{10,14},{3,7},{... | collective-permute-start | bytes 3145736 | tf_op jit(solution)/shard_map/ppermute | solution.py:27
  10.8 2.4 collective-permute-start.4
  13.2 21.1 %collective-permute-done.2 = bf16[256,2048]{1,0:T(8,128)(2,1)S(1)} collective-permute-done((bf16[256,2048]{1,0:T(8,128)(2,1)}, bf16[256,2048]{1,0:T(8,128)(2,1)S(1)}, u32[]{:S(2)}, u32[]{:S(2)}) %collective-permute-start.2) | collective-permute-done | bytes 1048608 | tf_op jit(solution)/shard_map/ppermute | solution.py:27
  34.3 3.5 %collective-permute-start.3 = (bf16[256,2048]{1,0:T(8,128)(2,1)S(1)}, bf16[256,2048]{1,0:T(8,128)(2,1)}, u32[]{:S(2)}, u32[]{:S(2)}) collective-permute-start(bf16[256,2048]{1,0:T(8,128)(2,1)S(1)} %collective-permute-done.2), channel_id=1, source_target_pairs={{4,8},{8,12},{5,9},{9,13},{6,10},{10,14},{7,11},{11,15},{20,24},{2... | collective-permute-start | bytes 3145736 | tf_op jit(solution)/shard_map/ppermute | solution.py:27
  37.8 4.4 %collective-permute-start.5 = (bf16[256,2048]{1,0:T(8,128)(2,1)}, bf16[256,2048]{1,0:T(8,128)(2,1)}, u32[]{:S(2)}, u32[]{:S(2)}) collective-permute-start(bf16[256,2048]{1,0:T(8,128)(2,1)} %collective-permute-done.4), channel_id=1, source_target_pairs={{4,0},{8,4},{5,1},{9,5},{6,2},{10,6},{7,3},{11,7},{20,16},{24,20},... | collective-permute-start | bytes 3145736 | tf_op jit(solution)/shard_map/ppermute | solution.py:28
  42.2 2.3 all-gather.2.cloned.1.call-done
  44.5 8.7 %convolution_convert_fusion.3 = bf16[512,2048]{1,0:T(8,128)(2,1)S(1)} fusion(bf16[2048,2048]{1,0:T(8,128)(2,1)} %param.6, bf16[1024,2048]{1,0:T(8,128)(2,1)} %all-gather.2.cloned.1.call-done), kind=kOutput, calls=%fused_computation.3 | convolution fusion | flops 4296015872 | bytes 12582912 | tf_op jit(solution)/shard_map/dot_general | solution.py:112
  53.2 1.1 constant_dynamic-slice_fusion.2
  54.3 4.8 %convolution_convert_fusion.2 = bf16[512,2048]{1,0:T(8,128)(2,1)S(1)} fusion(bf16[2048,2048]{1,0:T(8,128)(2,1)S(1)} %copy-done.10, bf16[1024,2048]{1,0:T(8,128)(2,1)S(1)} %copy-done.11), kind=kOutput, calls=%fused_computation.2 | convolution fusion | flops 4296015872 | bytes 12582912 | tf_op jit(solution)/shard_map/dot_general | solution.py:112
  59.1 1.2 constant_dynamic-slice_fusion
  60.4 2.4 collective-permute-done.5
  62.8 1.3 collective-permute-start.1
  64.1 1.5 collective-permute-start
  65.6 1.3 collective-permute-start.8
  66.8 1.5 collective-permute-start.6
  68.4 7.1 %collective-permute-start.11 = (bf16[256,2048]{1,0:T(8,128)(2,1)}, bf16[256,2048]{1,0:T(8,128)(2,1)}, u32[]{:S(2)}, u32[]{:S(2)}) collective-permute-start(bf16[256,2048]{1,0:T(8,128)(2,1)} %collective-permute-done.3), channel_id=1, source_target_pairs={{8,12},{9,13},{10,14},{11,15},{24,28},{25,29},{26,30},{27,31}} | collective-permute-start | bytes 3145736 | tf_op jit(solution)/shard_map/ppermute | solution.py:27
  75.5 1.3 broadcast_select_fusion.2
  76.8 5.8 %fusion = bf16[2048,512]{1,0:T(8,128)(2,1)} fusion(bf16[2048,2048]{1,0:T(8,128)(2,1)S(1)} %bitcast.9, bf16[256,2048]{1,0:T(8,128)(2,1)S(1)} %broadcast_select_fusion.2, bf16[256,2048]{1,0:T(8,128)(2,1)S(1)} %copy-done.12), kind=kOutput, calls=%fused_computation.4 | convolution fusion | flops 4300210176 | bytes 12582912 | tf_op jit(solution)/shard_map/dot_general | solution.py:102
  82.6 2.9 %add_convert_fusion.7 = (bf16[128,2048]{1,0:T(8,128)(2,1)}, bf16[128,2048]{1,0:T(8,128)(2,1)}) fusion(bf16[128,2048]{1,0:T(8,128)(2,1)} %collective-permute-done, bf16[512,2048]{1,0:T(8,128)(2,1)} %copy-done.7, s32[]{:T(128)S(6)} %select_n.112, s32[]{:T(128)S(6)} %select_n.113, bf16[128,2048]{1,0:T(8,128)(2,1)} %collective-permute-done.1), kind=kLoop, calls=%fused_computation.23 | loop fusion | flops 2097152 | bytes 3145736 | tf_op jit(solution)/shard_map/convert_element_type | solution.py:19
  85.5 1.3 collective-permute-start.12
  86.8 4.6 %collective-permute-start.14 = (bf16[128,2048]{1,0:T(8,128)(2,1)}, bf16[128,2048]{1,0:T(8,128)(2,1)}, u32[]{:S(2)}, u32[]{:S(2)}) collective-permute-start(bf16[128,2048]{1,0:T(8,128)(2,1)} %get-tuple-element.40), channel_id=1, source_target_pairs={{8,4},{12,8},{9,5},{13,9},{10,6},{14,10},{11,7},{15,11},{24,20},{2... | collective-permute-start | bytes 1572872 | tf_op jit(solution)/shard_map/ppermute | solution.py:53
  91.5 0.9 collective-permute-start.10
  92.4 2.6 %add_convert_fusion.8 = (bf16[128,2048]{1,0:T(8,128)(2,1)}, bf16[128,2048]{1,0:T(8,128)(2,1)}) fusion(bf16[128,2048]{1,0:T(8,128)(2,1)} %collective-permute-done.8, bf16[512,2048]{1,0:T(8,128)(2,1)S(1)} %convolution_convert_fusion.2, s32[]{:T(128)S(6)} %select_n.113, s32[]{:T(128)S(6)} %select_n.112, bf16[128,2048]{1,0:T(8,128)(2,1)} %collective-permute-done.6), kind=kLoop, calls=%fused_computation.26 | loop fusion | flops 2097152 | bytes 3145736 | tf_op jit(solution)/shard_map/convert_element_type | solution.py:19
  94.9 4.6 %collective-permute-start.9 = (bf16[128,2048]{1,0:T(8,128)(2,1)}, bf16[128,2048]{1,0:T(8,128)(2,1)}, u32[]{:S(2)}, u32[]{:S(2)}) collective-permute-start(bf16[128,2048]{1,0:T(8,128)(2,1)} %get-tuple-element.41), channel_id=1, source_target_pairs={{8,4},{12,8},{9,5},{13,9},{10,6},{14,10},{11,7},{15,11},{24,20},{2... | collective-permute-start | bytes 1572872 | tf_op jit(solution)/shard_map/ppermute | solution.py:53
  99.6 1.3 collective-permute-start.7
  100.9 3.2 %collective-permute-done.14 = bf16[128,2048]{1,0:T(8,128)(2,1)} collective-permute-done((bf16[128,2048]{1,0:T(8,128)(2,1)}, bf16[128,2048]{1,0:T(8,128)(2,1)}, u32[]{:S(2)}, u32[]{:S(2)}) %collective-permute-start.14) | collective-permute-done | bytes 524320 | tf_op jit(solution)/shard_map/ppermute | solution.py:53
  104.0 2.6 %add_convert_fusion.6 = (bf16[128,2048]{1,0:T(8,128)(2,1)}, bf16[128,2048]{1,0:T(8,128)(2,1)}) fusion(bf16[128,2048]{1,0:T(8,128)(2,1)} %collective-permute-done.12, bf16[512,2048]{1,0:T(8,128)(2,1)S(1)} %copy-done.8, s32[]{:T(128)S(6)} %select_n.121, s32[]{:T(128)S(6)} %select_n.122, bf16[128,2048]{1,0:T(8,128)(2,1)} %collective-permute-done.14), kind=kLoop, calls=%fused_computation.22 | loop fusion | flops 2097152 | bytes 3145736 | tf_op jit(solution)/shard_map/convert_element_type | solution.py:19
  106.6 1.9 collective-permute-start.13
  108.6 4.6 %collective-permute-start.15 = (bf16[128,2048]{1,0:T(8,128)(2,1)}, bf16[128,2048]{1,0:T(8,128)(2,1)}, u32[]{:S(2)}, u32[]{:S(2)}) collective-permute-start(bf16[128,2048]{1,0:T(8,128)(2,1)} %get-tuple-element.38), channel_id=1, source_target_pairs={{4,0},{8,4},{12,8},{5,1},{9,5},{13,9},{6,2},{10,6},{14,10},{7,3},{... | collective-permute-start | bytes 1572872 | tf_op jit(solution)/shard_map/ppermute | solution.py:53
  113.1 1.4 broadcast_select_fusion
  114.6 11.8 %fusion.1 = bf16[2048,512]{1,0:T(8,128)(2,1)} fusion(bf16[2048,2048]{1,0:T(8,128)(2,1)} %param.7, bf16[256,2048]{1,0:T(8,128)(2,1)S(1)} %broadcast_select_fusion, bf16[256,2048]{1,0:T(8,128)(2,1)S(1)} %broadcast_select_fusion.1), kind=kOutput, calls=%fused_computation.5 | convolution fusion | flops 4300210176 | bytes 12582912 | tf_op jit(solution)/shard_map/dot_general | solution.py:102
  126.5 1.6 add_convert_fusion.2
  128.1 2.1 collective-permute-start.22
  130.2 4.4 %collective-permute-start.23 = (bf16[128,2048]{1,0:T(8,128)(2,1)S(1)}, bf16[128,2048]{1,0:T(8,128)(2,1)S(1)}, u32[]{:S(2)}, u32[]{:S(2)}) collective-permute-start(bf16[128,2048]{1,0:T(8,128)(2,1)S(1)} %get-tuple-element.36), channel_id=1, source_target_pairs={{4,0},{8,4},{12,8},{5,1},{9,5},{13,9},{6,2},{10,6},{14,10},{7,3},{... | collective-permute-start | bytes 1572872 | tf_op jit(solution)/shard_map/ppermute | solution.py:53
  134.9 1.7 constant_dynamic-update-slice_fusion.1
  136.6 3.9 %collective-permute-start.17 = (bf16[128,2048]{1,0:T(8,128)(2,1)S(1)}, bf16[128,2048]{1,0:T(8,128)(2,1)}, u32[]{:S(2)}, u32[]{:S(2)}) collective-permute-start(bf16[128,2048]{1,0:T(8,128)(2,1)S(1)} %get-tuple-element.34), channel_id=1, source_target_pairs={{4,0},{8,4},{12,8},{5,1},{9,5},{13,9},{6,2},{10,6},{14,10},{7,3},{... | collective-permute-start | bytes 1572872 | tf_op jit(solution)/shard_map/ppermute | solution.py:28
  140.5 2.7 %collective-permute-start.16 = (bf16[128,2048]{1,0:T(8,128)(2,1)S(1)}, bf16[128,2048]{1,0:T(8,128)(2,1)}, u32[]{:S(2)}, u32[]{:S(2)}) collective-permute-start(bf16[128,2048]{1,0:T(8,128)(2,1)S(1)} %get-tuple-element.34), channel_id=1, source_target_pairs={{0,4},{4,8},{8,12},{1,5},{5,9},{9,13},{2,6},{6,10},{10,14},{3,7},{... | collective-permute-start | bytes 1572872 | tf_op jit(solution)/shard_map/ppermute | solution.py:27
  143.2 3.8 %collective-permute-done.23 = bf16[128,2048]{1,0:T(8,128)(2,1)S(1)} collective-permute-done((bf16[128,2048]{1,0:T(8,128)(2,1)S(1)}, bf16[128,2048]{1,0:T(8,128)(2,1)S(1)}, u32[]{:S(2)}, u32[]{:S(2)}) %collective-permute-start.23) | collective-permute-done | bytes 524320 | tf_op jit(solution)/shard_map/ppermute | solution.py:53
  147.2 1.3 constant_dynamic-update-slice_fusion
  148.6 1.9 collective-permute-start.24
  150.5 4.4 %collective-permute-start.25 = (bf16[128,2048]{1,0:T(8,128)(2,1)S(1)}, bf16[128,2048]{1,0:T(8,128)(2,1)}, u32[]{:S(2)}, u32[]{:S(2)}) collective-permute-start(bf16[128,2048]{1,0:T(8,128)(2,1)S(1)} %get-tuple-element.32), channel_id=1, source_target_pairs={{4,0},{8,4},{12,8},{5,1},{9,5},{13,9},{6,2},{10,6},{14,10},{7,3},{... | collective-permute-start | bytes 1572872 | tf_op jit(solution)/shard_map/ppermute | solution.py:28
  154.9 3.3 %collective-permute-done.17 = bf16[128,2048]{1,0:T(8,128)(2,1)} collective-permute-done((bf16[128,2048]{1,0:T(8,128)(2,1)S(1)}, bf16[128,2048]{1,0:T(8,128)(2,1)}, u32[]{:S(2)}, u32[]{:S(2)}) %collective-permute-start.17) | collective-permute-done | bytes 524320 | tf_op jit(solution)/shard_map/ppermute | solution.py:28
  158.2 5.3 %collective-permute-start.18 = (bf16[128,2048]{1,0:T(8,128)(2,1)}, bf16[128,2048]{1,0:T(8,128)(2,1)}, u32[]{:S(2)}, u32[]{:S(2)}) collective-permute-start(bf16[128,2048]{1,0:T(8,128)(2,1)} %collective-permute-done.17), channel_id=1, source_target_pairs={{4,0},{8,4},{5,1},{9,5},{6,2},{10,6},{7,3},{11,7},{20,16},{24,20},... | collective-permute-start | bytes 1572872 | tf_op jit(solution)/shard_map/ppermute | solution.py:28
  163.5 2.1 collective-permute-start.20
  165.6 2.8 %collective-permute-done.24 = bf16[128,2048]{1,0:T(8,128)(2,1)} collective-permute-done((bf16[128,2048]{1,0:T(8,128)(2,1)S(1)}, bf16[128,2048]{1,0:T(8,128)(2,1)}, u32[]{:S(2)}, u32[]{:S(2)}) %collective-permute-start.24) | collective-permute-done | bytes 524320 | tf_op jit(solution)/shard_map/ppermute | solution.py:27
  168.4 2.5 %collective-permute-start.28 = (bf16[128,2048]{1,0:T(8,128)(2,1)}, bf16[128,2048]{1,0:T(8,128)(2,1)S(1)}, u32[]{:S(2)}, u32[]{:S(2)}) collective-permute-start(bf16[128,2048]{1,0:T(8,128)(2,1)} %collective-permute-done.24), channel_id=1, source_target_pairs={{4,8},{8,12},{5,9},{9,13},{6,10},{10,14},{7,11},{11,15},{20,24},{2... | collective-permute-start | bytes 1572872 | tf_op jit(solution)/shard_map/ppermute | solution.py:27
  170.9 3.4 %collective-permute-start.26 = (bf16[128,2048]{1,0:T(8,128)(2,1)}, bf16[128,2048]{1,0:T(8,128)(2,1)S(1)}, u32[]{:S(2)}, u32[]{:S(2)}) collective-permute-start(bf16[128,2048]{1,0:T(8,128)(2,1)} %collective-permute-done.25), channel_id=1, source_target_pairs={{4,0},{8,4},{5,1},{9,5},{6,2},{10,6},{7,3},{11,7},{20,16},{24,20},... | collective-permute-start | bytes 1572872 | tf_op jit(solution)/shard_map/ppermute | solution.py:28
  174.3 6.3 %collective-permute-done.18 = bf16[128,2048]{1,0:T(8,128)(2,1)} collective-permute-done((bf16[128,2048]{1,0:T(8,128)(2,1)}, bf16[128,2048]{1,0:T(8,128)(2,1)}, u32[]{:S(2)}, u32[]{:S(2)}) %collective-permute-start.18) | collective-permute-done | bytes 524320 | tf_op jit(solution)/shard_map/ppermute | solution.py:28
  182.2 1.6 collective-permute-start.21
  183.8 5.8 %collective-permute-done.28 = bf16[128,2048]{1,0:T(8,128)(2,1)S(1)} collective-permute-done((bf16[128,2048]{1,0:T(8,128)(2,1)}, bf16[128,2048]{1,0:T(8,128)(2,1)S(1)}, u32[]{:S(2)}, u32[]{:S(2)}) %collective-permute-start.28) | collective-permute-done | bytes 524320 | tf_op jit(solution)/shard_map/ppermute | solution.py:27
  189.5 4.3 %collective-permute-start.29 = (bf16[128,2048]{1,0:T(8,128)(2,1)S(1)}, bf16[128,2048]{1,0:T(8,128)(2,1)S(1)}, u32[]{:S(2)}, u32[]{:S(2)}) collective-permute-start(bf16[128,2048]{1,0:T(8,128)(2,1)S(1)} %collective-permute-done.28), channel_id=1, source_target_pairs={{8,12},{9,13},{10,14},{11,15},{24,28},{25,29},{26,30},{27,31}} | collective-permute-start | bytes 1572872 | tf_op jit(solution)/shard_map/ppermute | solution.py:27
  194.6 1.2 select_dynamic-update-slice_fusion.5
  195.9 1.2 select_dynamic-update-slice_fusion.2
  197.3 2.4 collective-permute-done.21
  199.7 1.2 select_dynamic-update-slice_fusion.3.refs_0_
  200.9 1.4 copy-done.4
  202.3 3.1 %collective-permute-done.29 = bf16[128,2048]{1,0:T(8,128)(2,1)S(1)} collective-permute-done((bf16[128,2048]{1,0:T(8,128)(2,1)S(1)}, bf16[128,2048]{1,0:T(8,128)(2,1)S(1)}, u32[]{:S(2)}, u32[]{:S(2)}) %collective-permute-start.29) | collective-permute-done | bytes 524320 | tf_op jit(solution)/shard_map/ppermute | solution.py:27
  205.4 1.2 select_dynamic-update-slice_fusion.refs_1_
  206.5 8.6 %all-reduce.5.cloned.1.call-done = bf16[2048,512]{1,0:T(8,128)(2,1)} async-done(((bf16[2048,512]{1,0:T(8,128)(2,1)}), bf16[2048,512]{1,0:T(8,128)(2,1)}) %all-reduce.5.cloned.1.call-update) | async-done | bytes 2097168 | tf_op jit(solution)/shard_map/psum | solution.py:136
  215.1 2.4 slice_dynamic-update-slice_fusion.1
  217.6 2.3 slice_dynamic-update-slice_fusion.grads_ref
  219.8 2.2 copy-done.1
  222.0 20.2 %shard_map.46 = f32[2048,2048]{1,0:T(8,128)} custom-call(bf16[2048,1024]{1,0:T(8,128)(2,1)S(1)} %copy-done.1, bf16[512,2048]{1,0:T(8,128)(2,1)S(1)} %copy-done.5, bf16[512,2048]{1,0:T(8,128)(2,1)S(1)} %select_dynamic-update-slice_fusion.refs_1_), custom_call_target="tpu_custom_call" | custom-call | flops 17179869184 | bytes 25165824 | tf_op jit(solution)/shard_map/pallas_call | solution.py:84
  (65 shorter events, 3.5 us)
Async XLA Ops:
  6.5 38.0 %all-gather.2.cloned.1.call-start = ((), (), s32[]{:S(2)}) async-start(), calls=%async_computation | async-start | bytes 5242880 | tf_op jit(solution)/shard_map/all_gather | solution.py:108
  7.3 156.2 %all-reduce.3.cloned.1.call-start = ((), (), s32[]{:S(2)}) async-start(), calls=%async_computation.1 | async-start | bytes 4194304 | tf_op jit(solution)/shard_map/psum | solution.py:134
  7.3 27.0 %collective-permute-start.2 = (bf16[256,2048]{1,0:T(8,128)(2,1)}, bf16[256,2048]{1,0:T(8,128)(2,1)S(1)}, u32[]{:S(2)}, u32[]{:S(2)}) collective-permute-start(bf16[256,2048]{1,0:T(8,128)(2,1)} %param.5), channel_id=1, source_target_pairs={{0,4},{4,8},{8,12},{1,5},{5,9},{9,13},{2,6},{6,10},{10,14},{3,7},{... | collective-permute-start | bytes 3145736 | tf_op jit(solution)/shard_map/ppermute | solution.py:27
  10.8 27.0 %collective-permute-start.4 = (bf16[256,2048]{1,0:T(8,128)(2,1)}, bf16[256,2048]{1,0:T(8,128)(2,1)}, u32[]{:S(2)}, u32[]{:S(2)}) collective-permute-start(bf16[256,2048]{1,0:T(8,128)(2,1)} %param.5), channel_id=1, source_target_pairs={{4,0},{8,4},{12,8},{5,1},{9,5},{13,9},{6,2},{10,6},{14,10},{7,3},{... | collective-permute-start | bytes 3145736 | tf_op jit(solution)/shard_map/ppermute | solution.py:28
  34.3 26.1 %collective-permute-start.3 = (bf16[256,2048]{1,0:T(8,128)(2,1)S(1)}, bf16[256,2048]{1,0:T(8,128)(2,1)}, u32[]{:S(2)}, u32[]{:S(2)}) collective-permute-start(bf16[256,2048]{1,0:T(8,128)(2,1)S(1)} %collective-permute-done.2), channel_id=1, source_target_pairs={{4,8},{8,12},{5,9},{9,13},{6,10},{10,14},{7,11},{11,15},{20,24},{2... | collective-permute-start | bytes 3145736 | tf_op jit(solution)/shard_map/ppermute | solution.py:27
  37.8 25.0 %collective-permute-start.5 = (bf16[256,2048]{1,0:T(8,128)(2,1)}, bf16[256,2048]{1,0:T(8,128)(2,1)}, u32[]{:S(2)}, u32[]{:S(2)}) collective-permute-start(bf16[256,2048]{1,0:T(8,128)(2,1)} %collective-permute-done.4), channel_id=1, source_target_pairs={{4,0},{8,4},{5,1},{9,5},{6,2},{10,6},{7,3},{11,7},{20,16},{24,20},... | collective-permute-start | bytes 3145736 | tf_op jit(solution)/shard_map/ppermute | solution.py:28
  44.5 9.8 %copy-start.10 = (bf16[2048,2048]{1,0:T(8,128)(2,1)S(1)}, bf16[2048,2048]{1,0:T(8,128)(2,1)}, u32[]{:S(2)}) copy-start(bf16[2048,2048]{1,0:T(8,128)(2,1)} %param.6) | copy-start | bytes 25165828
  44.5 9.8 %copy-start.11 = (bf16[1024,2048]{1,0:T(8,128)(2,1)S(1)}, bf16[1024,2048]{1,0:T(8,128)(2,1)}, u32[]{:S(2)}) copy-start(bf16[1024,2048]{1,0:T(8,128)(2,1)} %all-gather.2.cloned.1.call-done) | copy-start | bytes 12582916
  53.2 5.9 %copy-start.7 = (bf16[512,2048]{1,0:T(8,128)(2,1)}, bf16[512,2048]{1,0:T(8,128)(2,1)S(1)}, u32[]{:S(2)}) copy-start(bf16[512,2048]{1,0:T(8,128)(2,1)S(1)} %convolution_convert_fusion.3) | copy-start | bytes 6291460
  53.2 23.6 %slice-start = ((s8[8388608]{0:T(1024)(128)(4,1)}), s8[4194304]{0:T(1024)(128)(4,1)S(1)}, s32[]{:S(2)}) async-start(s8[8388608]{0:T(1024)(128)(4,1)} %bitcast.8), calls=%async_computation.3 | async-start | bytes 8388608
  54.3 22.5 %slice-start.1 = ((s8[8388608]{0:T(1024)(128)(4,1)}), s8[4194304]{0:T(1024)(128)(4,1)S(1)}, s32[]{:S(2)}) async-start(s8[8388608]{0:T(1024)(128)(4,1)} %bitcast.8), calls=%async_computation.4 | async-start | bytes 8388608
  59.1 67.3 %copy-start.6 = (bf16[512,2048]{1,0:T(8,128)(2,1)}, bf16[512,2048]{1,0:T(8,128)(2,1)S(1)}, u32[]{:S(2)}) copy-start(bf16[512,2048]{1,0:T(8,128)(2,1)S(1)} %convolution_convert_fusion.2) | copy-start | bytes 6291460
  60.3 16.5 %copy-start.12 = (bf16[256,2048]{1,0:T(8,128)(2,1)S(1)}, bf16[256,2048]{1,0:T(8,128)(2,1)}, u32[]{:S(2)}) copy-start(bf16[256,2048]{1,0:T(8,128)(2,1)} %param.5) | copy-start | bytes 3145732
  62.8 19.8 %collective-permute-start.1 = (bf16[128,2048]{1,0:T(8,128)(2,1)}, bf16[128,2048]{1,0:T(8,128)(2,1)}, u32[]{:S(2)}, u32[]{:S(2)}) collective-permute-start(bf16[128,2048]{1,0:T(8,128)(2,1)} %get-tuple-element.45), channel_id=1, source_target_pairs={{12,8},{13,9},{14,10},{15,11},{28,24},{29,25},{30,26},{31,27}} | collective-permute-start | bytes 1572872 | tf_op jit(solution)/shard_map/ppermute | solution.py:53
  64.1 18.6 %collective-permute-start = (bf16[128,2048]{1,0:T(8,128)(2,1)}, bf16[128,2048]{1,0:T(8,128)(2,1)}, u32[]{:S(2)}, u32[]{:S(2)}) collective-permute-start(bf16[128,2048]{1,0:T(8,128)(2,1)} %get-tuple-element.46), channel_id=1, source_target_pairs={{0,4},{1,5},{2,6},{3,7},{16,20},{17,21},{18,22},{19,23}} | collective-permute-start | bytes 1572872 | tf_op jit(solution)/shard_map/ppermute | solution.py:52
  65.6 25.9 %collective-permute-start.8 = (bf16[128,2048]{1,0:T(8,128)(2,1)}, bf16[128,2048]{1,0:T(8,128)(2,1)}, u32[]{:S(2)}, u32[]{:S(2)}) collective-permute-start(bf16[128,2048]{1,0:T(8,128)(2,1)} %get-tuple-element.43), channel_id=1, source_target_pairs={{12,8},{13,9},{14,10},{15,11},{28,24},{29,25},{30,26},{31,27}} | collective-permute-start | bytes 1572872 | tf_op jit(solution)/shard_map/ppermute | solution.py:53
  66.8 25.5 %collective-permute-start.6 = (bf16[128,2048]{1,0:T(8,128)(2,1)}, bf16[128,2048]{1,0:T(8,128)(2,1)}, u32[]{:S(2)}, u32[]{:S(2)}) collective-permute-start(bf16[128,2048]{1,0:T(8,128)(2,1)} %get-tuple-element.44), channel_id=1, source_target_pairs={{0,4},{1,5},{2,6},{3,7},{16,20},{17,21},{18,22},{19,23}} | collective-permute-start | bytes 1572872 | tf_op jit(solution)/shard_map/ppermute | solution.py:52
  68.4 40.2 %collective-permute-start.11 = (bf16[256,2048]{1,0:T(8,128)(2,1)}, bf16[256,2048]{1,0:T(8,128)(2,1)}, u32[]{:S(2)}, u32[]{:S(2)}) collective-permute-start(bf16[256,2048]{1,0:T(8,128)(2,1)} %collective-permute-done.3), channel_id=1, source_target_pairs={{8,12},{9,13},{10,14},{11,15},{24,28},{25,29},{26,30},{27,31}} | collective-permute-start | bytes 3145736 | tf_op jit(solution)/shard_map/ppermute | solution.py:27
  85.5 14.0 %collective-permute-start.12 = (bf16[128,2048]{1,0:T(8,128)(2,1)}, bf16[128,2048]{1,0:T(8,128)(2,1)}, u32[]{:S(2)}, u32[]{:S(2)}) collective-permute-start(bf16[128,2048]{1,0:T(8,128)(2,1)} %get-tuple-element.39), channel_id=1, source_target_pairs={{0,4},{4,8},{1,5},{5,9},{2,6},{6,10},{3,7},{7,11},{16,20},{20,24},... | collective-permute-start | bytes 1572872 | tf_op jit(solution)/shard_map/ppermute | solution.py:52
  86.8 17.2 %collective-permute-start.14 = (bf16[128,2048]{1,0:T(8,128)(2,1)}, bf16[128,2048]{1,0:T(8,128)(2,1)}, u32[]{:S(2)}, u32[]{:S(2)}) collective-permute-start(bf16[128,2048]{1,0:T(8,128)(2,1)} %get-tuple-element.40), channel_id=1, source_target_pairs={{8,4},{12,8},{9,5},{13,9},{10,6},{14,10},{11,7},{15,11},{24,20},{2... | collective-permute-start | bytes 1572872 | tf_op jit(solution)/shard_map/ppermute | solution.py:53
  91.4 123.7 %all-reduce.5.cloned.1.call-start = ((), (), s32[]{:S(2)}) async-start(), calls=%async_computation.2 | async-start | bytes 4194304 | tf_op jit(solution)/shard_map/psum | solution.py:136
  91.5 12.6 %copy-start.8 = (bf16[512,2048]{1,0:T(8,128)(2,1)S(1)}, bf16[512,2048]{1,0:T(8,128)(2,1)}, u32[]{:S(2)}) copy-start(bf16[512,2048]{1,0:T(8,128)(2,1)} %copy-done.7) | copy-start | bytes 6291460
  91.5 23.0 %collective-permute-start.10 = (bf16[256,2048]{1,0:T(8,128)(2,1)}, bf16[256,2048]{1,0:T(8,128)(2,1)S(1)}, u32[]{:S(2)}, u32[]{:S(2)}) collective-permute-start(bf16[256,2048]{1,0:T(8,128)(2,1)} %collective-permute-done.5), channel_id=1, source_target_pairs={{4,0},{5,1},{6,2},{7,3},{20,16},{21,17},{22,18},{23,19}} | collective-permute-start | bytes 3145736 | tf_op jit(solution)/shard_map/ppermute | solution.py:28
  94.9 31.5 %collective-permute-start.9 = (bf16[128,2048]{1,0:T(8,128)(2,1)}, bf16[128,2048]{1,0:T(8,128)(2,1)}, u32[]{:S(2)}, u32[]{:S(2)}) collective-permute-start(bf16[128,2048]{1,0:T(8,128)(2,1)} %get-tuple-element.41), channel_id=1, source_target_pairs={{8,4},{12,8},{9,5},{13,9},{10,6},{14,10},{11,7},{15,11},{24,20},{2... | collective-permute-start | bytes 1572872 | tf_op jit(solution)/shard_map/ppermute | solution.py:53
  99.6 26.9 %collective-permute-start.7 = (bf16[128,2048]{1,0:T(8,128)(2,1)}, bf16[128,2048]{1,0:T(8,128)(2,1)}, u32[]{:S(2)}, u32[]{:S(2)}) collective-permute-start(bf16[128,2048]{1,0:T(8,128)(2,1)} %get-tuple-element.42), channel_id=1, source_target_pairs={{0,4},{4,8},{1,5},{5,9},{2,6},{6,10},{3,7},{7,11},{16,20},{20,24},... | collective-permute-start | bytes 1572872 | tf_op jit(solution)/shard_map/ppermute | solution.py:52
  106.6 28.0 %collective-permute-start.13 = (bf16[128,2048]{1,0:T(8,128)(2,1)}, bf16[128,2048]{1,0:T(8,128)(2,1)}, u32[]{:S(2)}, u32[]{:S(2)}) collective-permute-start(bf16[128,2048]{1,0:T(8,128)(2,1)} %get-tuple-element.37), channel_id=1, source_target_pairs={{0,4},{4,8},{8,12},{1,5},{5,9},{9,13},{2,6},{6,10},{10,14},{3,7},{... | collective-permute-start | bytes 1572872 | tf_op jit(solution)/shard_map/ppermute | solution.py:52
  108.6 26.1 %collective-permute-start.15 = (bf16[128,2048]{1,0:T(8,128)(2,1)}, bf16[128,2048]{1,0:T(8,128)(2,1)}, u32[]{:S(2)}, u32[]{:S(2)}) collective-permute-start(bf16[128,2048]{1,0:T(8,128)(2,1)} %get-tuple-element.38), channel_id=1, source_target_pairs={{4,0},{8,4},{12,8},{5,1},{9,5},{13,9},{6,2},{10,6},{14,10},{7,3},{... | collective-permute-start | bytes 1572872 | tf_op jit(solution)/shard_map/ppermute | solution.py:53
  128.1 15.1 %collective-permute-start.22 = (bf16[128,2048]{1,0:T(8,128)(2,1)S(1)}, bf16[128,2048]{1,0:T(8,128)(2,1)S(1)}, u32[]{:S(2)}, u32[]{:S(2)}) collective-permute-start(bf16[128,2048]{1,0:T(8,128)(2,1)S(1)} %get-tuple-element.35), channel_id=1, source_target_pairs={{0,4},{4,8},{8,12},{1,5},{5,9},{9,13},{2,6},{6,10},{10,14},{3,7},{... | collective-permute-start | bytes 1572872 | tf_op jit(solution)/shard_map/ppermute | solution.py:52
  130.2 16.8 %collective-permute-start.23 = (bf16[128,2048]{1,0:T(8,128)(2,1)S(1)}, bf16[128,2048]{1,0:T(8,128)(2,1)S(1)}, u32[]{:S(2)}, u32[]{:S(2)}) collective-permute-start(bf16[128,2048]{1,0:T(8,128)(2,1)S(1)} %get-tuple-element.36), channel_id=1, source_target_pairs={{4,0},{8,4},{12,8},{5,1},{9,5},{13,9},{6,2},{10,6},{14,10},{7,3},{... | collective-permute-start | bytes 1572872 | tf_op jit(solution)/shard_map/ppermute | solution.py:53
  136.6 12.0 %copy-start.2 = (bf16[512,2048]{1,0:T(8,128)(2,1)}, bf16[512,2048]{1,0:T(8,128)(2,1)S(1)}, u32[]{:S(2)}) copy-start(bf16[512,2048]{1,0:T(8,128)(2,1)S(1)} %get-tuple-element.33) | copy-start | bytes 6291460
  136.6 21.6 %collective-permute-start.17 = (bf16[128,2048]{1,0:T(8,128)(2,1)S(1)}, bf16[128,2048]{1,0:T(8,128)(2,1)}, u32[]{:S(2)}, u32[]{:S(2)}) collective-permute-start(bf16[128,2048]{1,0:T(8,128)(2,1)S(1)} %get-tuple-element.34), channel_id=1, source_target_pairs={{4,0},{8,4},{12,8},{5,1},{9,5},{13,9},{6,2},{10,6},{14,10},{7,3},{... | collective-permute-start | bytes 1572872 | tf_op jit(solution)/shard_map/ppermute | solution.py:28
  140.5 23.0 %collective-permute-start.16 = (bf16[128,2048]{1,0:T(8,128)(2,1)S(1)}, bf16[128,2048]{1,0:T(8,128)(2,1)}, u32[]{:S(2)}, u32[]{:S(2)}) collective-permute-start(bf16[128,2048]{1,0:T(8,128)(2,1)S(1)} %get-tuple-element.34), channel_id=1, source_target_pairs={{0,4},{4,8},{8,12},{1,5},{5,9},{9,13},{2,6},{6,10},{10,14},{3,7},{... | collective-permute-start | bytes 1572872 | tf_op jit(solution)/shard_map/ppermute | solution.py:27
  148.6 19.8 %collective-permute-start.24 = (bf16[128,2048]{1,0:T(8,128)(2,1)S(1)}, bf16[128,2048]{1,0:T(8,128)(2,1)}, u32[]{:S(2)}, u32[]{:S(2)}) collective-permute-start(bf16[128,2048]{1,0:T(8,128)(2,1)S(1)} %get-tuple-element.32), channel_id=1, source_target_pairs={{0,4},{4,8},{8,12},{1,5},{5,9},{9,13},{2,6},{6,10},{10,14},{3,7},{... | collective-permute-start | bytes 1572872 | tf_op jit(solution)/shard_map/ppermute | solution.py:27
  150.5 20.4 %collective-permute-start.25 = (bf16[128,2048]{1,0:T(8,128)(2,1)S(1)}, bf16[128,2048]{1,0:T(8,128)(2,1)}, u32[]{:S(2)}, u32[]{:S(2)}) collective-permute-start(bf16[128,2048]{1,0:T(8,128)(2,1)S(1)} %get-tuple-element.32), channel_id=1, source_target_pairs={{4,0},{8,4},{12,8},{5,1},{9,5},{13,9},{6,2},{10,6},{14,10},{7,3},{... | collective-permute-start | bytes 1572872 | tf_op jit(solution)/shard_map/ppermute | solution.py:28
  158.2 22.4 %collective-permute-start.18 = (bf16[128,2048]{1,0:T(8,128)(2,1)}, bf16[128,2048]{1,0:T(8,128)(2,1)}, u32[]{:S(2)}, u32[]{:S(2)}) collective-permute-start(bf16[128,2048]{1,0:T(8,128)(2,1)} %collective-permute-done.17), channel_id=1, source_target_pairs={{4,0},{8,4},{5,1},{9,5},{6,2},{10,6},{7,3},{11,7},{20,16},{24,20},... | collective-permute-start | bytes 1572872 | tf_op jit(solution)/shard_map/ppermute | solution.py:28
  163.5 18.3 %copy-start.9 = (bf16[2048,512]{1,0:T(8,128)(2,1)S(1)}, bf16[2048,512]{1,0:T(8,128)(2,1)}, u32[]{:S(2)}) copy-start(bf16[2048,512]{1,0:T(8,128)(2,1)} %all-reduce.3.cloned.1.call-done) | copy-start | bytes 6291460
  163.5 18.6 %collective-permute-start.20 = (bf16[128,2048]{1,0:T(8,128)(2,1)}, bf16[128,2048]{1,0:T(8,128)(2,1)S(1)}, u32[]{:S(2)}, u32[]{:S(2)}) collective-permute-start(bf16[128,2048]{1,0:T(8,128)(2,1)} %collective-permute-done.16), channel_id=1, source_target_pairs={{4,8},{8,12},{5,9},{9,13},{6,10},{10,14},{7,11},{11,15},{20,24},{2... | collective-permute-start | bytes 1572872 | tf_op jit(solution)/shard_map/ppermute | solution.py:27
  168.4 21.2 %collective-permute-start.28 = (bf16[128,2048]{1,0:T(8,128)(2,1)}, bf16[128,2048]{1,0:T(8,128)(2,1)S(1)}, u32[]{:S(2)}, u32[]{:S(2)}) collective-permute-start(bf16[128,2048]{1,0:T(8,128)(2,1)} %collective-permute-done.24), channel_id=1, source_target_pairs={{4,8},{8,12},{5,9},{9,13},{6,10},{10,14},{7,11},{11,15},{20,24},{2... | collective-permute-start | bytes 1572872 | tf_op jit(solution)/shard_map/ppermute | solution.py:27
  170.9 22.9 %collective-permute-start.26 = (bf16[128,2048]{1,0:T(8,128)(2,1)}, bf16[128,2048]{1,0:T(8,128)(2,1)S(1)}, u32[]{:S(2)}, u32[]{:S(2)}) collective-permute-start(bf16[128,2048]{1,0:T(8,128)(2,1)} %collective-permute-done.25), channel_id=1, source_target_pairs={{4,0},{8,4},{5,1},{9,5},{6,2},{10,6},{7,3},{11,7},{20,16},{24,20},... | collective-permute-start | bytes 1572872 | tf_op jit(solution)/shard_map/ppermute | solution.py:28
  180.6 14.0 %collective-permute-start.19 = (bf16[128,2048]{1,0:T(8,128)(2,1)}, bf16[128,2048]{1,0:T(8,128)(2,1)S(1)}, u32[]{:S(2)}, u32[]{:S(2)}) collective-permute-start(bf16[128,2048]{1,0:T(8,128)(2,1)} %collective-permute-done.18), channel_id=1, source_target_pairs={{4,0},{5,1},{6,2},{7,3},{20,16},{21,17},{22,18},{23,19}} | collective-permute-start | bytes 1572872 | tf_op jit(solution)/shard_map/ppermute | solution.py:28
  181.8 12.7 %copy-start.3 = (bf16[512,2048]{1,0:T(8,128)(2,1)S(1)}, bf16[512,2048]{1,0:T(8,128)(2,1)}, u32[]{:S(2)}) copy-start(bf16[512,2048]{1,0:T(8,128)(2,1)} %copy-done.2) | copy-start | bytes 6291460
  182.1 15.0 %copy-start = (bf16[2048,1024]{1,0:T(8,128)(2,1)}, bf16[2048,1024]{1,0:T(8,128)(2,1)S(1)}, u32[]{:S(2)}) copy-start(bf16[2048,1024]{1,0:T(8,128)(2,1)S(1)} %slice_dynamic-update-slice_fusion.2) | copy-start | bytes 12582916
  182.2 17.6 %collective-permute-start.21 = (bf16[128,2048]{1,0:T(8,128)(2,1)S(1)}, bf16[128,2048]{1,0:T(8,128)(2,1)S(1)}, u32[]{:S(2)}, u32[]{:S(2)}) collective-permute-start(bf16[128,2048]{1,0:T(8,128)(2,1)S(1)} %collective-permute-done.20), channel_id=1, source_target_pairs={{8,12},{9,13},{10,14},{11,15},{24,28},{25,29},{26,30},{27,31}} | collective-permute-start | bytes 1572872 | tf_op jit(solution)/shard_map/ppermute | solution.py:27
  189.5 15.8 %collective-permute-start.29 = (bf16[128,2048]{1,0:T(8,128)(2,1)S(1)}, bf16[128,2048]{1,0:T(8,128)(2,1)S(1)}, u32[]{:S(2)}, u32[]{:S(2)}) collective-permute-start(bf16[128,2048]{1,0:T(8,128)(2,1)S(1)} %collective-permute-done.28), channel_id=1, source_target_pairs={{8,12},{9,13},{10,14},{11,15},{24,28},{25,29},{26,30},{27,31}} | collective-permute-start | bytes 1572872 | tf_op jit(solution)/shard_map/ppermute | solution.py:27
  193.8 2.1 collective-permute-start.27
  200.9 1.4 copy-start.4
  215.1 4.7 %copy-start.5 = (bf16[512,2048]{1,0:T(8,128)(2,1)S(1)}, bf16[512,2048]{1,0:T(8,128)(2,1)}, u32[]{:S(2)}) copy-start(bf16[512,2048]{1,0:T(8,128)(2,1)} %copy-done.4) | copy-start | bytes 6291460
  219.8 2.2 copy-start.1
Sparse Core Ops, SparseCore 0:
  8.9 35.5 all-gather.1
  91.5 51.4 all-reduce.2
  163.6 51.4 all-reduce.4
